TPU v7x, 32 devices: a whole 2x2x4 slice. The times are simulated.
32 devices in a mesh: section: 4 (over z), dp: 8 (over y, x, core).
Axes of the slice: x: 2, y: 2, z: 4, core: 2. Of those that a mesh axis runs over, the one named last changes fastest.
Arguments:
- out_grad: bfloat16 [2, 512, 6144], P(None, 'dp'), may hold values from -6 to 6
- x_rows: bfloat16 [4, 2, 16, 6144], P('section'), may hold values from -6 to 6
- saved_u: bfloat16 [4, 2, 16, 5376], P('section', None, None, 'dp'), may hold values from -6 to 6
- w_up_t: bfloat16 [4, 5376, 6144], P('section', 'dp'), may hold values from -0.078125 to 0.078125
- w_down: bfloat16 [4, 5376, 6144], P('section', 'dp'), may hold values from -0.078125 to 0.078125
- gate: float32 [4, 2, 16], P('section', None, 'dp'), may hold values from 0.2 to 1
- route_tokens: int32 [4, 2, 16], P('section', None, 'dp'), may hold values from 0 to 63
- route_count: int32 [4, 2, 8], P('section', None, 'dp'), may hold values from 1 to 2, as said below
Outputs:
- in_grad: bfloat16 [4, 2, 512, 6144], P('section', None, 'dp')
- grad_up_t: bfloat16 [4, 5376, 6144], P('section', 'dp')
- grad_down: bfloat16 [4, 5376, 6144], P('section', 'dp')
Inputs may be any that keep to these rules, and one draw needn't show every extreme that they name: `route_tokens`: a token index within the micro-batch rows of the slot's dp index. `route_count`: in every layer and micro-batch some dp index has all 2 slots live.
All inputs are finite; a program needn't handle non-finite values.
Results may differ from a plain program's by a relative error of at most 0.0059.
Values may be sent and summed in bfloat16 or wider, within the bound.
A program may use at most 128 MiB of HBM per device.

v0:
```python
import jax
import jax.numpy as jnp
from jax import lax
from jax.sharding import PartitionSpec as P


def from_behind(block, axis, distance):
    devices = range(lax.axis_size(axis))
    route = [(i - distance, i) for i in devices if i - distance in devices]
    return lax.ppermute(block, axis, route)


def silu_pair(pre_activation):
    sigmoid_v = jax.nn.sigmoid(pre_activation)
    return (pre_activation * sigmoid_v, sigmoid_v * (1.0 + pre_activation * (1.0 - sigmoid_v)))


def per_device(out_grad, x_rows, saved_u, w_up_t, w_down, gate, route_tokens, route_count):
    section_count = lax.axis_size("section")
    dp_count = lax.axis_size("dp")
    section_index = lax.axis_index("section")
    micro_count = out_grad.shape[0]
    tok_rows = out_grad.shape[1]
    feature_count = out_grad.shape[2]
    slot_count = gate.shape[2]
    hid_rows = w_down.shape[1]
    tick_count = micro_count + section_count - 1
    down_proj = w_down[0]
    up_weights = w_up_t[0]
    is_top = section_index == section_count - 1
    incoming = jnp.zeros((tok_rows, feature_count), jnp.bfloat16)
    init_state = (
        incoming,
        jnp.zeros((micro_count, tok_rows, feature_count), jnp.bfloat16),
        jnp.zeros((hid_rows, feature_count), jnp.float32),
        jnp.zeros((hid_rows, feature_count), jnp.float32),
    )

    def tick_step(tick_index, loop_state):
        received, in_grad, grad_down, grad_up = loop_state
        micro_index = tick_index - (section_count - 1 - section_index)
        valid_tick = (micro_index >= 0) & (micro_index < micro_count)
        micro_pick = jnp.clip(micro_index, 0, micro_count - 1)
        top_grad = out_grad[micro_pick]
        grad_slab = jnp.where(is_top, top_grad, received)
        grad_slab = jnp.where(valid_tick, grad_slab, jnp.zeros_like(grad_slab))
        token_ids = route_tokens[0, micro_pick]
        live_count = route_count[0, micro_pick, 0]
        live_slots = jnp.arange(slot_count) < live_count
        weights = jnp.where(live_slots & valid_tick, gate[0, micro_pick], jnp.float32(0.0))
        scaled = (weights[:, None] * grad_slab[token_ids].astype(jnp.float32)).astype(jnp.bfloat16)
        activation_f, slope_factor = silu_pair(saved_u[0, micro_pick].astype(jnp.float32))
        activation = activation_f.astype(jnp.bfloat16)
        row_piece = lax.all_gather(scaled, "dp", axis=0, tiled=True)
        down_total = grad_down
        product = jnp.einsum("rd,hd->rh", row_piece, down_proj, preferred_element_type=jnp.float32)
        hidden_back = product
        down_total = down_total + jnp.einsum(
            "rh,rd->hd", activation, row_piece, preferred_element_type=jnp.float32
        )
        hidden_back, grad_down = (hidden_back, down_total)
        hidden_grad = (hidden_back * slope_factor).astype(jnp.bfloat16)
        grad_up = grad_up + jnp.einsum(
            "rh,rd->hd", hidden_grad, x_rows[0, micro_pick], preferred_element_type=jnp.float32
        )
        partial_value = jnp.dot(hidden_grad, up_weights, preferred_element_type=jnp.float32)
        partial_value = partial_value.reshape(dp_count, slot_count, feature_count)
        swapped = lax.all_to_all(partial_value, "dp", split_axis=0, concat_axis=0, tiled=True)
        own_rows = jnp.sum(swapped, axis=0)
        new_slab = grad_slab.astype(jnp.float32).at[token_ids].add(own_rows).astype(jnp.bfloat16)
        in_grad = jnp.where(
            valid_tick, lax.dynamic_update_index_in_dim(in_grad, new_slab, micro_pick, 0), in_grad
        )
        outgoing = from_behind(new_slab, "section", -1)
        return (outgoing, in_grad, grad_down, grad_up)

    final_state = lax.fori_loop(0, tick_count, tick_step, init_state)
    in_grad = final_state[1]
    grad_down = final_state[2]
    grad_up = final_state[3]
    return (in_grad[None], grad_up.astype(jnp.bfloat16)[None], grad_down.astype(jnp.bfloat16)[None])


def solution(mesh):
    return jax.shard_map(
        per_device,
        mesh=mesh,
        in_specs=(
            P(None, "dp", None),
            P("section", None, None, None),
            P("section", None, None, "dp"),
            P("section", "dp", None),
            P("section", "dp", None),
            P("section", None, "dp"),
            P("section", None, "dp"),
            P("section", None, "dp"),
        ),
        out_specs=(
            P("section", None, "dp", None),
            P("section", "dp", None),
            P("section", "dp", None),
        ),
        check_vma=False,
    )
```

profile of v0, /device:TPU:0, one launch (start us, length us, event | category | flops | bytes accessed | tf_op | source)
XLA Modules:
  0.0 341.5 jit_solution(1775081397892592770)
XLA Ops:
  0.7 1.3 broadcast_in_dim.35
  2.0 321.8 %while.22 = (s32[]{:T(128)}, bf16[64,6144]{1,0:T(8,128)(2,1)S(1)}, bf16[2,64,6144]{2,1,0:T(8,128)(2,1)}, f32[672,6144]{1,0:T(8,128)}, f32[672,6144]{1,0:T(8,128)...) while((s32[]{:T(128)}, bf16[64,6144]{1,0:T(8,128)(2,1)S(1)}, ...), condition=%wide.region_3.4_spmd.clone, body=%wide.region_0.3_spmd.clone.sunk | while | flops 547271680 | bytes 131154400 | solution.py:77
  3.9 1.3 and_select_fusion.2
  5.3 1.3 fusion.53
  7.3 10.7 %all-gather.3 = bf16[8,2,6144]{2,1,0:T(2,128)(2,1)S(1)} all-gather(bf16[1,2,6144]{2,1,0:T(2,128)(2,1)S(1)} %fusion.55), channel_id=1, replica_groups=mesh['section'=4,'dp'=8] {'dp'}, dimensions={0}, use_global_device_ids=true | all-gather | bytes 221184 | tf_op jit(solution)/shard_map/while/body/eval_jaxpr/all_gather | solution.py:54
  18.1 5.7 %fusion.56 = bf16[16,672]{1,0:T(8,128)(2,1)S(1)} fusion(bf16[16,6144]{1,0:T(8,128)(2,1)S(1)} %reshape.103, bf16[672,6144]{1,0:T(8,128)(2,1)} %get-tuple-element.578, bf16[1,2,16,672]{3,2,1,0:T(8,128)(2,1)} %get-tuple-element.579, s32[]{:T(128)S(6)} %min.12), kind=kOutput, calls=%fused_computation.5.clone.1 | convolution fusion | flops 132228096 | bytes 8497156 | tf_op jit(solution)/shard_map/while/body/eval_jaxpr/rd,hd->rh/dot_general | solution.py:56
  26.0 3.5 %all-to-all-start = ((f32[8,2,6144]{2,1,0:T(2,128)}), f32[8,2,6144]{2,1,0:T(2,128)S(1)}, u32[]{:S(2)}, u32[]{:S(2)}) async-start(f32[8,2,6144]{2,1,0:T(2,128)} %reshape.104), calls=%async_computation | async-start | bytes 786432 | tf_op jit(solution)/shard_map/while/body/eval_jaxpr/all_to_all | solution.py:68
  29.5 8.0 %select_add_fusion.4 = f32[672,6144]{1,0:T(8,128)} fusion(f32[672,6144]{1,0:T(8,128)} %get-tuple-element.551, bf16[16,6144]{1,0:T(8,128)(2,1)S(1)} %reshape.103, pred[]{:T(512)S(6)} %compare.3, bf16[1,2,16,672]{3,2,1,0:T(8,128)(2,1)S(1)} %copy-done.1, s32[]{:T(128)S(6)} %min.12), kind=kOutput, calls=%fused_computation.3.clone.1 | convolution fusion | flops 140442624 | bytes 33251332 | tf_op jit(solution)/shard_map/while/body/eval_jaxpr/rh,rd->hd/dot_general | solution.py:58
  39.1 2.2 fusion.58
  42.7 8.9 %select_add_fusion.5 = f32[672,6144]{1,0:T(8,128)} fusion(f32[672,6144]{1,0:T(8,128)} %get-tuple-element.552, bf16[16,672]{1,0:T(8,128)(2,1)S(1)} %fusion.56, pred[]{:T(512)S(6)} %compare.3, bf16[1,2,16,6144]{3,2,1,0:T(8,128)(2,1)} %get-tuple-element.581, s32[]{:T(128)S(6)} %min.12), kind=kOutput, calls=%fused_computation.2.clone.1 | convolution fusion | flops 140378112 | bytes 33248260 | tf_op jit(solution)/shard_map/while/body/eval_jaxpr/rh,rd->hd/dot_general | solution.py:63
  51.6 11.2 %collective-permute-done = bf16[64,6144]{1,0:T(8,128)(2,1)S(1)} collective-permute-done((bf16[64,6144]{1,0:T(8,128)(2,1)S(1)}, bf16[64,6144]{1,0:T(8,128)(2,1)S(1)}, u32[]{:S(2)}, u32[]{:S(2)}) %collective-permute-start) | collective-permute-done | bytes 786464 | tf_op jit(solution)/shard_map/while/body/eval_jaxpr/ppermute | solution.py:10
  64.8 1.3 and_select_fusion.2
  66.1 1.3 fusion.53
  68.1 9.4 %all-gather.3 = bf16[8,2,6144]{2,1,0:T(2,128)(2,1)S(1)} all-gather(bf16[1,2,6144]{2,1,0:T(2,128)(2,1)S(1)} %fusion.55), channel_id=1, replica_groups=mesh['section'=4,'dp'=8] {'dp'}, dimensions={0}, use_global_device_ids=true | all-gather | bytes 221184 | tf_op jit(solution)/shard_map/while/body/eval_jaxpr/all_gather | solution.py:54
  77.6 5.7 %fusion.56 = bf16[16,672]{1,0:T(8,128)(2,1)S(1)} fusion(bf16[16,6144]{1,0:T(8,128)(2,1)S(1)} %reshape.103, bf16[672,6144]{1,0:T(8,128)(2,1)} %get-tuple-element.578, bf16[1,2,16,672]{3,2,1,0:T(8,128)(2,1)} %get-tuple-element.579, s32[]{:T(128)S(6)} %min.12), kind=kOutput, calls=%fused_computation.5.clone.1 | convolution fusion | flops 132228096 | bytes 8497156 | tf_op jit(solution)/shard_map/while/body/eval_jaxpr/rd,hd->rh/dot_general | solution.py:56
  85.6 3.5 %all-to-all-start = ((f32[8,2,6144]{2,1,0:T(2,128)}), f32[8,2,6144]{2,1,0:T(2,128)S(1)}, u32[]{:S(2)}, u32[]{:S(2)}) async-start(f32[8,2,6144]{2,1,0:T(2,128)} %reshape.104), calls=%async_computation | async-start | bytes 786432 | tf_op jit(solution)/shard_map/while/body/eval_jaxpr/all_to_all | solution.py:68
  89.0 13.7 %select_add_fusion.4 = f32[672,6144]{1,0:T(8,128)} fusion(f32[672,6144]{1,0:T(8,128)} %get-tuple-element.551, bf16[16,6144]{1,0:T(8,128)(2,1)S(1)} %reshape.103, pred[]{:T(512)S(6)} %compare.3, bf16[1,2,16,672]{3,2,1,0:T(8,128)(2,1)S(1)} %copy-done.1, s32[]{:T(128)S(6)} %min.12), kind=kOutput, calls=%fused_computation.3.clone.1 | convolution fusion | flops 140442624 | bytes 33251332 | tf_op jit(solution)/shard_map/while/body/eval_jaxpr/rh,rd->hd/dot_general | solution.py:58
  104.2 2.2 fusion.58
  107.7 13.8 %select_add_fusion.5 = f32[672,6144]{1,0:T(8,128)} fusion(f32[672,6144]{1,0:T(8,128)} %get-tuple-element.552, bf16[16,672]{1,0:T(8,128)(2,1)S(1)} %fusion.56, pred[]{:T(512)S(6)} %compare.3, bf16[1,2,16,6144]{3,2,1,0:T(8,128)(2,1)} %get-tuple-element.581, s32[]{:T(128)S(6)} %min.12), kind=kOutput, calls=%fused_computation.2.clone.1 | convolution fusion | flops 140378112 | bytes 33248260 | tf_op jit(solution)/shard_map/while/body/eval_jaxpr/rh,rd->hd/dot_general | solution.py:63
  121.5 6.6 %collective-permute-done = bf16[64,6144]{1,0:T(8,128)(2,1)S(1)} collective-permute-done((bf16[64,6144]{1,0:T(8,128)(2,1)S(1)}, bf16[64,6144]{1,0:T(8,128)(2,1)S(1)}, u32[]{:S(2)}, u32[]{:S(2)}) %collective-permute-start) | collective-permute-done | bytes 786464 | tf_op jit(solution)/shard_map/while/body/eval_jaxpr/ppermute | solution.py:10
  130.0 1.3 and_select_fusion.2
  131.4 1.3 fusion.53
  133.3 9.4 %all-gather.3 = bf16[8,2,6144]{2,1,0:T(2,128)(2,1)S(1)} all-gather(bf16[1,2,6144]{2,1,0:T(2,128)(2,1)S(1)} %fusion.55), channel_id=1, replica_groups=mesh['section'=4,'dp'=8] {'dp'}, dimensions={0}, use_global_device_ids=true | all-gather | bytes 221184 | tf_op jit(solution)/shard_map/while/body/eval_jaxpr/all_gather | solution.py:54
  142.9 5.7 %fusion.56 = bf16[16,672]{1,0:T(8,128)(2,1)S(1)} fusion(bf16[16,6144]{1,0:T(8,128)(2,1)S(1)} %reshape.103, bf16[672,6144]{1,0:T(8,128)(2,1)} %get-tuple-element.578, bf16[1,2,16,672]{3,2,1,0:T(8,128)(2,1)} %get-tuple-element.579, s32[]{:T(128)S(6)} %min.12), kind=kOutput, calls=%fused_computation.5.clone.1 | convolution fusion | flops 132228096 | bytes 8497156 | tf_op jit(solution)/shard_map/while/body/eval_jaxpr/rd,hd->rh/dot_general | solution.py:56
  150.8 3.5 %all-to-all-start = ((f32[8,2,6144]{2,1,0:T(2,128)}), f32[8,2,6144]{2,1,0:T(2,128)S(1)}, u32[]{:S(2)}, u32[]{:S(2)}) async-start(f32[8,2,6144]{2,1,0:T(2,128)} %reshape.104), calls=%async_computation | async-start | bytes 786432 | tf_op jit(solution)/shard_map/while/body/eval_jaxpr/all_to_all | solution.py:68
  154.3 13.7 %select_add_fusion.4 = f32[672,6144]{1,0:T(8,128)} fusion(f32[672,6144]{1,0:T(8,128)} %get-tuple-element.551, bf16[16,6144]{1,0:T(8,128)(2,1)S(1)} %reshape.103, pred[]{:T(512)S(6)} %compare.3, bf16[1,2,16,672]{3,2,1,0:T(8,128)(2,1)S(1)} %copy-done.1, s32[]{:T(128)S(6)} %min.12), kind=kOutput, calls=%fused_computation.3.clone.1 | convolution fusion | flops 140442624 | bytes 33251332 | tf_op jit(solution)/shard_map/while/body/eval_jaxpr/rh,rd->hd/dot_general | solution.py:58
  169.4 2.2 fusion.58
  172.9 13.8 %select_add_fusion.5 = f32[672,6144]{1,0:T(8,128)} fusion(f32[672,6144]{1,0:T(8,128)} %get-tuple-element.552, bf16[16,672]{1,0:T(8,128)(2,1)S(1)} %fusion.56, pred[]{:T(512)S(6)} %compare.3, bf16[1,2,16,6144]{3,2,1,0:T(8,128)(2,1)} %get-tuple-element.581, s32[]{:T(128)S(6)} %min.12), kind=kOutput, calls=%fused_computation.2.clone.1 | convolution fusion | flops 140378112 | bytes 33248260 | tf_op jit(solution)/shard_map/while/body/eval_jaxpr/rh,rd->hd/dot_general | solution.py:63
  186.7 6.6 %collective-permute-done = bf16[64,6144]{1,0:T(8,128)(2,1)S(1)} collective-permute-done((bf16[64,6144]{1,0:T(8,128)(2,1)S(1)}, bf16[64,6144]{1,0:T(8,128)(2,1)S(1)}, u32[]{:S(2)}, u32[]{:S(2)}) %collective-permute-start) | collective-permute-done | bytes 786464 | tf_op jit(solution)/shard_map/while/body/eval_jaxpr/ppermute | solution.py:10
  195.3 1.3 and_select_fusion.2
  196.6 1.3 fusion.53
  198.6 9.4 %all-gather.3 = bf16[8,2,6144]{2,1,0:T(2,128)(2,1)S(1)} all-gather(bf16[1,2,6144]{2,1,0:T(2,128)(2,1)S(1)} %fusion.55), channel_id=1, replica_groups=mesh['section'=4,'dp'=8] {'dp'}, dimensions={0}, use_global_device_ids=true | all-gather | bytes 221184 | tf_op jit(solution)/shard_map/while/body/eval_jaxpr/all_gather | solution.py:54
  208.1 5.7 %fusion.56 = bf16[16,672]{1,0:T(8,128)(2,1)S(1)} fusion(bf16[16,6144]{1,0:T(8,128)(2,1)S(1)} %reshape.103, bf16[672,6144]{1,0:T(8,128)(2,1)} %get-tuple-element.578, bf16[1,2,16,672]{3,2,1,0:T(8,128)(2,1)} %get-tuple-element.579, s32[]{:T(128)S(6)} %min.12), kind=kOutput, calls=%fused_computation.5.clone.1 | convolution fusion | flops 132228096 | bytes 8497156 | tf_op jit(solution)/shard_map/while/body/eval_jaxpr/rd,hd->rh/dot_general | solution.py:56
  216.1 3.5 %all-to-all-start = ((f32[8,2,6144]{2,1,0:T(2,128)}), f32[8,2,6144]{2,1,0:T(2,128)S(1)}, u32[]{:S(2)}, u32[]{:S(2)}) async-start(f32[8,2,6144]{2,1,0:T(2,128)} %reshape.104), calls=%async_computation | async-start | bytes 786432 | tf_op jit(solution)/shard_map/while/body/eval_jaxpr/all_to_all | solution.py:68
  219.5 13.7 %select_add_fusion.4 = f32[672,6144]{1,0:T(8,128)} fusion(f32[672,6144]{1,0:T(8,128)} %get-tuple-element.551, bf16[16,6144]{1,0:T(8,128)(2,1)S(1)} %reshape.103, pred[]{:T(512)S(6)} %compare.3, bf16[1,2,16,672]{3,2,1,0:T(8,128)(2,1)S(1)} %copy-done.1, s32[]{:T(128)S(6)} %min.12), kind=kOutput, calls=%fused_computation.3.clone.1 | convolution fusion | flops 140442624 | bytes 33251332 | tf_op jit(solution)/shard_map/while/body/eval_jaxpr/rh,rd->hd/dot_general | solution.py:58
  234.7 2.2 fusion.58
  238.2 13.8 %select_add_fusion.5 = f32[672,6144]{1,0:T(8,128)} fusion(f32[672,6144]{1,0:T(8,128)} %get-tuple-element.552, bf16[16,672]{1,0:T(8,128)(2,1)S(1)} %fusion.56, pred[]{:T(512)S(6)} %compare.3, bf16[1,2,16,6144]{3,2,1,0:T(8,128)(2,1)} %get-tuple-element.581, s32[]{:T(128)S(6)} %min.12), kind=kOutput, calls=%fused_computation.2.clone.1 | convolution fusion | flops 140378112 | bytes 33248260 | tf_op jit(solution)/shard_map/while/body/eval_jaxpr/rh,rd->hd/dot_general | solution.py:63
  252.0 6.6 %collective-permute-done = bf16[64,6144]{1,0:T(8,128)(2,1)S(1)} collective-permute-done((bf16[64,6144]{1,0:T(8,128)(2,1)S(1)}, bf16[64,6144]{1,0:T(8,128)(2,1)S(1)}, u32[]{:S(2)}, u32[]{:S(2)}) %collective-permute-start) | collective-permute-done | bytes 786464 | tf_op jit(solution)/shard_map/while/body/eval_jaxpr/ppermute | solution.py:10
  260.5 1.3 and_select_fusion.2
  261.9 1.3 fusion.53
  263.8 9.4 %all-gather.3 = bf16[8,2,6144]{2,1,0:T(2,128)(2,1)S(1)} all-gather(bf16[1,2,6144]{2,1,0:T(2,128)(2,1)S(1)} %fusion.55), channel_id=1, replica_groups=mesh['section'=4,'dp'=8] {'dp'}, dimensions={0}, use_global_device_ids=true | all-gather | bytes 221184 | tf_op jit(solution)/shard_map/while/body/eval_jaxpr/all_gather | solution.py:54
  273.4 5.7 %fusion.56 = bf16[16,672]{1,0:T(8,128)(2,1)S(1)} fusion(bf16[16,6144]{1,0:T(8,128)(2,1)S(1)} %reshape.103, bf16[672,6144]{1,0:T(8,128)(2,1)} %get-tuple-element.578, bf16[1,2,16,672]{3,2,1,0:T(8,128)(2,1)} %get-tuple-element.579, s32[]{:T(128)S(6)} %min.12), kind=kOutput, calls=%fused_computation.5.clone.1 | convolution fusion | flops 132228096 | bytes 8497156 | tf_op jit(solution)/shard_map/while/body/eval_jaxpr/rd,hd->rh/dot_general | solution.py:56
  281.3 3.5 %all-to-all-start = ((f32[8,2,6144]{2,1,0:T(2,128)}), f32[8,2,6144]{2,1,0:T(2,128)S(1)}, u32[]{:S(2)}, u32[]{:S(2)}) async-start(f32[8,2,6144]{2,1,0:T(2,128)} %reshape.104), calls=%async_computation | async-start | bytes 786432 | tf_op jit(solution)/shard_map/while/body/eval_jaxpr/all_to_all | solution.py:68
  284.8 13.7 %select_add_fusion.4 = f32[672,6144]{1,0:T(8,128)} fusion(f32[672,6144]{1,0:T(8,128)} %get-tuple-element.551, bf16[16,6144]{1,0:T(8,128)(2,1)S(1)} %reshape.103, pred[]{:T(512)S(6)} %compare.3, bf16[1,2,16,672]{3,2,1,0:T(8,128)(2,1)S(1)} %copy-done.1, s32[]{:T(128)S(6)} %min.12), kind=kOutput, calls=%fused_computation.3.clone.1 | convolution fusion | flops 140442624 | bytes 33251332 | tf_op jit(solution)/shard_map/while/body/eval_jaxpr/rh,rd->hd/dot_general | solution.py:58
  299.9 2.2 fusion.58
  303.4 13.8 %select_add_fusion.5 = f32[672,6144]{1,0:T(8,128)} fusion(f32[672,6144]{1,0:T(8,128)} %get-tuple-element.552, bf16[16,672]{1,0:T(8,128)(2,1)S(1)} %fusion.56, pred[]{:T(512)S(6)} %compare.3, bf16[1,2,16,6144]{3,2,1,0:T(8,128)(2,1)} %get-tuple-element.581, s32[]{:T(128)S(6)} %min.12), kind=kOutput, calls=%fused_computation.2.clone.1 | convolution fusion | flops 140378112 | bytes 33248260 | tf_op jit(solution)/shard_map/while/body/eval_jaxpr/rh,rd->hd/dot_general | solution.py:63
  317.2 6.6 %collective-permute-done = bf16[64,6144]{1,0:T(8,128)(2,1)S(1)} collective-permute-done((bf16[64,6144]{1,0:T(8,128)(2,1)S(1)}, bf16[64,6144]{1,0:T(8,128)(2,1)S(1)}, u32[]{:S(2)}, u32[]{:S(2)}) %collective-permute-start) | collective-permute-done | bytes 786464 | tf_op jit(solution)/shard_map/while/body/eval_jaxpr/ppermute | solution.py:10
  323.8 17.7 %convert_bitcast_fusion = (bf16[1,672,6144]{2,1,0:T(8,128)(2,1)}, bf16[1,672,6144]{2,1,0:T(8,128)(2,1)}) fusion(f32[672,6144]{1,0:T(8,128)} %get-tuple-element.345, f32[672,6144]{1,0:T(8,128)} %get-tuple-element.344), kind=kLoop, calls=%fused_computation.38 | loop fusion | flops 8257536 | bytes 49545216 | tf_op jit(solution)/shard_map/broadcast_in_dim | solution.py:81
  (83 shorter events, 38.0 us)
Async XLA Ops:
  18.1 5.8 %copy-start = (bf16[672,6144]{1,0:T(8,128)(2,1)S(1)}, bf16[672,6144]{1,0:T(8,128)(2,1)}, u32[]{:S(2)}) copy-start(bf16[672,6144]{1,0:T(8,128)(2,1)} %get-tuple-element.580) | copy-start | bytes 24772612 | tf_op jit(solution)/shard_map/while
  23.8 5.7 %copy-start.1 = (bf16[1,2,16,672]{3,2,1,0:T(8,128)(2,1)S(1)}, bf16[1,2,16,672]{3,2,1,0:T(8,128)(2,1)}, u32[]{:S(2)}) copy-start(bf16[1,2,16,672]{3,2,1,0:T(8,128)(2,1)} %get-tuple-element.579) | copy-start | bytes 129028 | tf_op jit(solution)/shard_map/while
  26.0 11.7 %all-to-all-start = ((f32[8,2,6144]{2,1,0:T(2,128)}), f32[8,2,6144]{2,1,0:T(2,128)S(1)}, u32[]{:S(2)}, u32[]{:S(2)}) async-start(f32[8,2,6144]{2,1,0:T(2,128)} %reshape.104), calls=%async_computation | async-start | bytes 786432 | tf_op jit(solution)/shard_map/while/body/eval_jaxpr/all_to_all | solution.py:68
  41.4 21.5 %collective-permute-start = (bf16[64,6144]{1,0:T(8,128)(2,1)S(1)}, bf16[64,6144]{1,0:T(8,128)(2,1)S(1)}, u32[]{:S(2)}, u32[]{:S(2)}) collective-permute-start(bf16[64,6144]{1,0:T(8,128)(2,1)S(1)} %get-tuple-element.527), channel_id=1, source_target_pairs={{8,0},{16,8},{24,16},{9,1},{17,9},{25,17},{10,2},{18,10},{26,18},{... | collective-permute-start | bytes 2359304 | tf_op jit(solution)/shard_map/while/body/eval_jaxpr/ppermute | solution.py:10
  77.6 5.8 %copy-start = (bf16[672,6144]{1,0:T(8,128)(2,1)S(1)}, bf16[672,6144]{1,0:T(8,128)(2,1)}, u32[]{:S(2)}) copy-start(bf16[672,6144]{1,0:T(8,128)(2,1)} %get-tuple-element.580) | copy-start | bytes 24772612 | tf_op jit(solution)/shard_map/while
  83.4 5.7 %copy-start.1 = (bf16[1,2,16,672]{3,2,1,0:T(8,128)(2,1)S(1)}, bf16[1,2,16,672]{3,2,1,0:T(8,128)(2,1)}, u32[]{:S(2)}) copy-start(bf16[1,2,16,672]{3,2,1,0:T(8,128)(2,1)} %get-tuple-element.579) | copy-start | bytes 129028 | tf_op jit(solution)/shard_map/while
  85.6 17.2 %all-to-all-start = ((f32[8,2,6144]{2,1,0:T(2,128)}), f32[8,2,6144]{2,1,0:T(2,128)S(1)}, u32[]{:S(2)}, u32[]{:S(2)}) async-start(f32[8,2,6144]{2,1,0:T(2,128)} %reshape.104), calls=%async_computation | async-start | bytes 786432 | tf_op jit(solution)/shard_map/while/body/eval_jaxpr/all_to_all | solution.py:68
  106.4 21.7 %collective-permute-start = (bf16[64,6144]{1,0:T(8,128)(2,1)S(1)}, bf16[64,6144]{1,0:T(8,128)(2,1)S(1)}, u32[]{:S(2)}, u32[]{:S(2)}) collective-permute-start(bf16[64,6144]{1,0:T(8,128)(2,1)S(1)} %get-tuple-element.527), channel_id=1, source_target_pairs={{8,0},{16,8},{24,16},{9,1},{17,9},{25,17},{10,2},{18,10},{26,18},{... | collective-permute-start | bytes 2359304 | tf_op jit(solution)/shard_map/while/body/eval_jaxpr/ppermute | solution.py:10
  142.9 5.8 %copy-start = (bf16[672,6144]{1,0:T(8,128)(2,1)S(1)}, bf16[672,6144]{1,0:T(8,128)(2,1)}, u32[]{:S(2)}) copy-start(bf16[672,6144]{1,0:T(8,128)(2,1)} %get-tuple-element.580) | copy-start | bytes 24772612 | tf_op jit(solution)/shard_map/while
  148.6 5.7 %copy-start.1 = (bf16[1,2,16,672]{3,2,1,0:T(8,128)(2,1)S(1)}, bf16[1,2,16,672]{3,2,1,0:T(8,128)(2,1)}, u32[]{:S(2)}) copy-start(bf16[1,2,16,672]{3,2,1,0:T(8,128)(2,1)} %get-tuple-element.579) | copy-start | bytes 129028 | tf_op jit(solution)/shard_map/while
  150.8 17.2 %all-to-all-start = ((f32[8,2,6144]{2,1,0:T(2,128)}), f32[8,2,6144]{2,1,0:T(2,128)S(1)}, u32[]{:S(2)}, u32[]{:S(2)}) async-start(f32[8,2,6144]{2,1,0:T(2,128)} %reshape.104), calls=%async_computation | async-start | bytes 786432 | tf_op jit(solution)/shard_map/while/body/eval_jaxpr/all_to_all | solution.py:68
  171.6 21.7 %collective-permute-start = (bf16[64,6144]{1,0:T(8,128)(2,1)S(1)}, bf16[64,6144]{1,0:T(8,128)(2,1)S(1)}, u32[]{:S(2)}, u32[]{:S(2)}) collective-permute-start(bf16[64,6144]{1,0:T(8,128)(2,1)S(1)} %get-tuple-element.527), channel_id=1, source_target_pairs={{8,0},{16,8},{24,16},{9,1},{17,9},{25,17},{10,2},{18,10},{26,18},{... | collective-permute-start | bytes 2359304 | tf_op jit(solution)/shard_map/while/body/eval_jaxpr/ppermute | solution.py:10
  208.1 5.8 %copy-start = (bf16[672,6144]{1,0:T(8,128)(2,1)S(1)}, bf16[672,6144]{1,0:T(8,128)(2,1)}, u32[]{:S(2)}) copy-start(bf16[672,6144]{1,0:T(8,128)(2,1)} %get-tuple-element.580) | copy-start | bytes 24772612 | tf_op jit(solution)/shard_map/while
  213.9 5.7 %copy-start.1 = (bf16[1,2,16,672]{3,2,1,0:T(8,128)(2,1)S(1)}, bf16[1,2,16,672]{3,2,1,0:T(8,128)(2,1)}, u32[]{:S(2)}) copy-start(bf16[1,2,16,672]{3,2,1,0:T(8,128)(2,1)} %get-tuple-element.579) | copy-start | bytes 129028 | tf_op jit(solution)/shard_map/while
  216.1 17.2 %all-to-all-start = ((f32[8,2,6144]{2,1,0:T(2,128)}), f32[8,2,6144]{2,1,0:T(2,128)S(1)}, u32[]{:S(2)}, u32[]{:S(2)}) async-start(f32[8,2,6144]{2,1,0:T(2,128)} %reshape.104), calls=%async_computation | async-start | bytes 786432 | tf_op jit(solution)/shard_map/while/body/eval_jaxpr/all_to_all | solution.py:68
  236.9 21.7 %collective-permute-start = (bf16[64,6144]{1,0:T(8,128)(2,1)S(1)}, bf16[64,6144]{1,0:T(8,128)(2,1)S(1)}, u32[]{:S(2)}, u32[]{:S(2)}) collective-permute-start(bf16[64,6144]{1,0:T(8,128)(2,1)S(1)} %get-tuple-element.527), channel_id=1, source_target_pairs={{8,0},{16,8},{24,16},{9,1},{17,9},{25,17},{10,2},{18,10},{26,18},{... | collective-permute-start | bytes 2359304 | tf_op jit(solution)/shard_map/while/body/eval_jaxpr/ppermute | solution.py:10
  273.4 5.8 %copy-start = (bf16[672,6144]{1,0:T(8,128)(2,1)S(1)}, bf16[672,6144]{1,0:T(8,128)(2,1)}, u32[]{:S(2)}) copy-start(bf16[672,6144]{1,0:T(8,128)(2,1)} %get-tuple-element.580) | copy-start | bytes 24772612 | tf_op jit(solution)/shard_map/while
  279.1 5.7 %copy-start.1 = (bf16[1,2,16,672]{3,2,1,0:T(8,128)(2,1)S(1)}, bf16[1,2,16,672]{3,2,1,0:T(8,128)(2,1)}, u32[]{:S(2)}) copy-start(bf16[1,2,16,672]{3,2,1,0:T(8,128)(2,1)} %get-tuple-element.579) | copy-start | bytes 129028 | tf_op jit(solution)/shard_map/while
  281.3 17.2 %all-to-all-start = ((f32[8,2,6144]{2,1,0:T(2,128)}), f32[8,2,6144]{2,1,0:T(2,128)S(1)}, u32[]{:S(2)}, u32[]{:S(2)}) async-start(f32[8,2,6144]{2,1,0:T(2,128)} %reshape.104), calls=%async_computation | async-start | bytes 786432 | tf_op jit(solution)/shard_map/while/body/eval_jaxpr/all_to_all | solution.py:68
  302.1 21.7 %collective-permute-start = (bf16[64,6144]{1,0:T(8,128)(2,1)S(1)}, bf16[64,6144]{1,0:T(8,128)(2,1)S(1)}, u32[]{:S(2)}, u32[]{:S(2)}) collective-permute-start(bf16[64,6144]{1,0:T(8,128)(2,1)S(1)} %get-tuple-element.527), channel_id=1, source_target_pairs={{8,0},{16,8},{24,16},{9,1},{17,9},{25,17},{10,2},{18,10},{26,18},{... | collective-permute-start | bytes 2359304 | tf_op jit(solution)/shard_map/while/body/eval_jaxpr/ppermute | solution.py:10
where the time goes:
time: 343 us; the launch traced here: 342 us
  matrix products  162 us (47%)
  other arithmetic  52.8 us (15%)
  blocking collectives  48.5 us (14%)
  waiting for transfers between devices  37.9 us (11%)
  starting transfers between devices  23.7 us (7%)
  local copies, waits for them, and re-layouts  15.8 us (5%)
    dot_general x5, matrix products, tick_step(): jnp.einsum('rh,rd->hd', hidden_grad, x_rows[0, micro_pick], preferred_ele...  64.2 us
    dot_general x5, matrix products, tick_step(): jnp.einsum('rh,rd->hd', activation, row_piece, preferred_element_type=jnp...  62.8 us
    all_gather x5, blocking collectives, tick_step(): row_piece = lax.all_gather(scaled, 'dp', axis=0, tiled=True)  48.5 us
    ppermute x5, waiting for transfers between devices, from_behind(): return lax.ppermute(block, axis, route)  37.6 us
    dot_general x5, matrix products, tick_step(): jnp.einsum('rd,hd->rh', row_piece, down_proj, preferred_element_type=jnp....  28.7 us
    broadcast_in_dim x1, other arithmetic, per_device(): grad_down.astype(jnp.bfloat16)[None]  17.7 us
    all_to_all x5, starting transfers between devices, tick_step(): lax.all_to_all(partial_value, 'dp', split_axis=0, concat_axis=0, tiled=True)  17.3 us
    select_n x5, other arithmetic, tick_step(): jnp.where(valid_tick, lax.dynamic_update_index_in_dim(in_grad, new_slab,...  11.1 us
  transfers between devices with their start and end apart: 10, of which 6 were waited for; matrix products, arithmetic and copies ran while one was open for 37% of the time, Pallas kernels for 0%

commit v1 on v0

v1 whole, which is shorter than its diff:
```python
import functools

import jax
import jax.numpy as jnp
from jax import lax
from jax.experimental import pallas as pl
from jax.experimental.pallas import tpu as pltpu
from jax.sharding import PartitionSpec as P

MESH = pl.DeviceIdType.MESH
TILE_ROWS = 16
GATHER_CHUNKS = 2
REDUCE_CHUNKS = 3


def chain_kernel(
    sizes,
    base_ref, weight_ref, id_col_ref, id_row_ref, id_send_ref, slope_ref, w_up_hbm, w_down_hbm,
    all_new_ref, all_ids_ref, gathered_ref, hidden_ref,
    w_up, w_down, gbuf, send_buf, recv_buf, new_buf, id_buf, cur_buf,
    weight_sem, gather_send, gather_recv, reduce_send, reduce_recv, id_send, id_recv, new_send, new_recv,
):
    sections, peers, fold, slots = sizes
    section = lax.axis_index("section")
    me = lax.axis_index("dp")
    width = gbuf.shape[1]
    hid = w_down.shape[0]
    rows = peers * TILE_ROWS

    down_copy = pltpu.make_async_copy(w_down_hbm, w_down, weight_sem.at[0])
    up_copy = pltpu.make_async_copy(w_up_hbm, w_up, weight_sem.at[1])
    down_copy.start()
    up_copy.start()

    def peer_at(k):
        return lax.rem(me + k, peers)

    barrier = pltpu.get_barrier_semaphore()

    def greet(k, carry):
        pl.semaphore_signal(barrier, inc=1, device_id=(section, peer_at(k)), device_id_type=MESH)
        return carry

    lax.fori_loop(1, peers, greet, 0)
    for k in range(1, sections):
        other = lax.rem(section + k, sections)
        pl.semaphore_signal(barrier, inc=1, device_id=(other, me), device_id_type=MESH)
    pl.semaphore_wait(barrier, peers - 1 + sections - 1)

    def id_copy(source, target):
        return pltpu.make_async_remote_copy(
            src_ref=id_send_ref, dst_ref=id_buf.at[source],
            send_sem=id_send.at[target], recv_sem=id_recv.at[source],
            device_id=(target, me), device_id_type=MESH)

    def new_copy(source, target):
        return pltpu.make_async_remote_copy(
            src_ref=new_buf.at[source], dst_ref=new_buf.at[source],
            send_sem=new_send.at[target], recv_sem=new_recv.at[source],
            device_id=(target, me), device_id_type=MESH)

    for target in range(sections - 1):
        @pl.when(target < section)
        def _():
            id_copy(section, target).start()

    cur_buf[...] = base_ref[...]
    id_col = id_col_ref[...]
    for upper in range(sections - 1, 0, -1):
        @pl.when(upper > section)
        def _():
            id_copy(upper, upper).wait_recv()
            new_copy(upper, upper).wait_recv()
            same = id_col[:, :TILE_ROWS] == id_buf[upper][:1, :TILE_ROWS]
            picks = jnp.where(same, 1.0, 0.0)
            hit = jnp.max(picks, axis=1, keepdims=True) > 0.5
            taken = jnp.dot(picks.astype(jnp.bfloat16), new_buf[upper], preferred_element_type=jnp.float32)
            cur_buf[...] = jnp.where(hit, taken, cur_buf[...].astype(jnp.float32)).astype(jnp.bfloat16)

    current = cur_buf[...].astype(jnp.float32)
    scaled = (weight_ref[...][:, :1] * current).astype(jnp.bfloat16)
    my_rows = pl.ds(pl.multiple_of(me * TILE_ROWS, TILE_ROWS), TILE_ROWS)
    gbuf[my_rows, :] = scaled

    g_width = width // GATHER_CHUNKS

    def gather_copy(chunk, source, target):
        place = (pl.ds(pl.multiple_of(source * TILE_ROWS, TILE_ROWS), TILE_ROWS), pl.ds(chunk * g_width, g_width))
        return pltpu.make_async_remote_copy(
            src_ref=gbuf.at[place], dst_ref=gbuf.at[place],
            send_sem=gather_send.at[chunk, target], recv_sem=gather_recv.at[chunk, source],
            device_id=(section, target), device_id_type=MESH)

    for chunk in range(GATHER_CHUNKS):
        def send(k, carry):
            gather_copy(chunk, me, peer_at(k)).start()
            return carry
        lax.fori_loop(1, peers, send, 0)

    down_copy.wait()
    lane_piece = lax.broadcasted_iota(jnp.int32, (hid, rows), 1) % TILE_ROWS // slots
    total = jnp.zeros((hid, rows), jnp.float32)
    for chunk in range(GATHER_CHUNKS):
        def arrive(k, carry):
            peer = peer_at(k)
            gather_copy(chunk, peer, peer).wait_recv()
            return carry
        lax.fori_loop(1, peers, arrive, 0)
        block = gbuf[:, chunk * g_width:(chunk + 1) * g_width]
        for piece in range(fold):
            start = piece * width + chunk * g_width
            product = lax.dot_general(
                w_down[:, start:start + g_width], block, (((1,), (1,)), ((), ())),
                preferred_element_type=jnp.float32)
            total = total + jnp.where(lane_piece == piece, product, 0.0)

    back = total.T.reshape(peers, TILE_ROWS, hid)
    summed = back
    for k in range(1, fold):
        cut = k * slots
        summed = summed + jnp.concatenate([back[:, cut:], back[:, :cut]], axis=1)
    hidden = (summed.reshape(rows, hid) * slope_ref[...]).astype(jnp.bfloat16)
    hidden_ref[...] = hidden

    r_width = width // REDUCE_CHUNKS

    def reduce_copy(chunk, source, target):
        columns = pl.ds(chunk * r_width, r_width)
        return pltpu.make_async_remote_copy(
            src_ref=send_buf.at[pl.ds(pl.multiple_of(target * TILE_ROWS, TILE_ROWS), TILE_ROWS), columns],
            dst_ref=recv_buf.at[pl.ds(pl.multiple_of(source * TILE_ROWS, TILE_ROWS), TILE_ROWS), columns],
            send_sem=reduce_send.at[chunk, target], recv_sem=reduce_recv.at[chunk, source],
            device_id=(section, target), device_id_type=MESH)

    up_copy.wait()
    row_piece = lax.broadcasted_iota(jnp.int32, (rows, r_width), 0) % TILE_ROWS // slots
    for chunk in range(REDUCE_CHUNKS):
        partial = jnp.zeros((rows, r_width), jnp.float32)
        for piece in range(fold):
            start = piece * width + chunk * r_width
            product = jnp.dot(hidden, w_up[:, start:start + r_width], preferred_element_type=jnp.float32)
            partial = jnp.where(row_piece == piece, product, partial)
        columns = slice(chunk * r_width, (chunk + 1) * r_width)
        send_buf[:, columns] = partial.astype(jnp.bfloat16)
        def send(k, carry):
            reduce_copy(chunk, me, peer_at(k)).start()
            return carry
        lax.fori_loop(1, peers, send, 0)
        recv_buf[my_rows, columns] = send_buf[my_rows, columns]

    for chunk in range(REDUCE_CHUNKS):
        def arrive(k, carry):
            peer = peer_at(k)
            reduce_copy(chunk, peer, peer).wait_recv()
            return carry
        lax.fori_loop(1, peers, arrive, 0)

    alike = jnp.where(id_col[:, :1] == id_row_ref[...][:1, :], 1.0, 0.0).astype(jnp.bfloat16)
    delta = jnp.dot(alike, recv_buf[...], preferred_element_type=jnp.float32)
    new_buf[section] = (current + delta).astype(jnp.bfloat16)
    for target in range(sections - 2, -1, -1):
        @pl.when(target < section)
        def _():
            new_copy(section, target).start()

    for layer in range(sections):
        @pl.when(layer > section)
        def _():
            all_new_ref[layer] = new_buf[layer]
            all_ids_ref[layer] = id_buf[layer]

        @pl.when(layer < section)
        def _():
            all_new_ref[layer] = jnp.zeros((TILE_ROWS, width), jnp.bfloat16)
            all_ids_ref[layer] = jnp.full(id_send_ref.shape, -1, jnp.int32)
    all_new_ref[section] = new_buf[section]
    all_ids_ref[section] = id_send_ref[...]
    gathered_ref[...] = gbuf[...]

    def drain(k, carry):
        peer = peer_at(k)
        for chunk in range(GATHER_CHUNKS):
            gather_copy(chunk, me, peer).wait_send()
        for chunk in range(REDUCE_CHUNKS):
            reduce_copy(chunk, me, peer).wait_send()
        return carry

    lax.fori_loop(1, peers, drain, 0)
    for target in range(sections - 1):
        @pl.when(target < section)
        def _():
            id_copy(section, target).wait_send()
            new_copy(section, target).wait_send()


def per_device(sections, peers, out_grad, x_rows, saved_u, w_up_t, w_down, gate, route_tokens, route_count):
    micro, tokens, features = out_grad.shape
    cap = gate.shape[2]
    slots = micro * cap
    fold = TILE_ROWS // slots
    width = features // fold
    hid = w_down.shape[1]
    rows = peers * TILE_ROWS

    token_ids = route_tokens[0]
    live = jnp.arange(cap)[None, :] < route_count[0]
    weights = jnp.where(live, gate[0], jnp.float32(0.0)).reshape(slots)
    base = out_grad[jnp.arange(micro)[:, None], token_ids].reshape(slots, fold, width)
    base = base.transpose(1, 0, 2).reshape(TILE_ROWS, width)
    flat_ids = (token_ids + tokens * jnp.arange(micro)[:, None]).reshape(slots)
    earlier = jnp.arange(slots)[None, :] < jnp.arange(slots)[:, None]
    repeat = jnp.any((flat_ids[:, None] == flat_ids[None, :]) & earlier, axis=1)
    piece_ids = (jnp.arange(fold)[:, None] * (micro * tokens) + flat_ids[None, :]).reshape(TILE_ROWS)
    sent_ids = jnp.where(jnp.tile(repeat, fold), -1, piece_ids)
    id_col = jnp.broadcast_to(piece_ids[:, None], (TILE_ROWS, 128))
    id_row = jnp.broadcast_to(jnp.tile(piece_ids, peers)[None, :], (8, rows))
    id_send = jnp.broadcast_to(jnp.concatenate([sent_ids, jnp.full(128 - TILE_ROWS, -1, jnp.int32)])[None, :], (8, 128))
    weight_col = jnp.broadcast_to(jnp.tile(weights, fold)[:, None], (TILE_ROWS, 128))

    pre = saved_u[0].astype(jnp.float32)
    sigmoid = jax.nn.sigmoid(pre)
    activation = (pre * sigmoid).astype(jnp.bfloat16).reshape(micro * peers * cap, hid)
    slope = sigmoid * (1.0 + pre * (1.0 - sigmoid))
    slope = slope.reshape(micro, peers, cap, hid).transpose(1, 0, 2, 3).reshape(peers, 1, slots, hid)
    slope = jnp.broadcast_to(slope, (peers, fold, slots, hid)).reshape(rows, hid)

    vmem = pl.BlockSpec(memory_space=pltpu.VMEM)
    dma = pltpu.SemaphoreType.DMA
    all_new, all_ids, gathered, hidden = pl.pallas_call(
        functools.partial(chain_kernel, (sections, peers, fold, slots)),
        out_shape=(
            jax.ShapeDtypeStruct((sections, TILE_ROWS, width), jnp.bfloat16),
            jax.ShapeDtypeStruct((sections, 8, 128), jnp.int32),
            jax.ShapeDtypeStruct((rows, width), jnp.bfloat16),
            jax.ShapeDtypeStruct((rows, hid), jnp.bfloat16),
        ),
        in_specs=[vmem] * 6 + [pl.BlockSpec(memory_space=pl.ANY)] * 2,
        out_specs=(vmem,) * 4,
        scratch_shapes=[
            pltpu.VMEM((hid, features), jnp.bfloat16),
            pltpu.VMEM((hid, features), jnp.bfloat16),
            pltpu.VMEM((rows, width), jnp.bfloat16),
            pltpu.VMEM((rows, width), jnp.bfloat16),
            pltpu.VMEM((rows, width), jnp.bfloat16),
            pltpu.VMEM((sections, TILE_ROWS, width), jnp.bfloat16),
            pltpu.VMEM((sections, 8, 128), jnp.int32),
            pltpu.VMEM((TILE_ROWS, width), jnp.bfloat16),
            dma((2,)),
            dma((GATHER_CHUNKS, peers)),
            dma((GATHER_CHUNKS, peers)),
            dma((REDUCE_CHUNKS, peers)),
            dma((REDUCE_CHUNKS, peers)),
            dma((sections,)),
            dma((sections,)),
            dma((sections,)),
            dma((sections,)),
        ],
        compiler_params=pltpu.CompilerParams(
            collective_id=0, has_side_effects=True, vmem_limit_bytes=48 * 1024 * 1024),
    )(base, weight_col, id_col, id_row, id_send, slope, w_up_t[0], w_down[0])

    hidden = hidden.reshape(peers, fold, micro, cap, hid)[:, 0].transpose(1, 0, 2, 3).reshape(-1, hid)
    scaled = gathered.reshape(peers, fold, micro, cap, width).transpose(2, 0, 3, 1, 4).reshape(-1, features)
    grad_down = jnp.einsum("rh,rd->hd", activation, scaled, preferred_element_type=jnp.float32)
    grad_up = jnp.einsum(
        "rh,rd->hd", hidden, x_rows[0].reshape(-1, features), preferred_element_type=jnp.float32)

    token = jnp.arange(micro * tokens, dtype=jnp.int32)[:, None]
    in_grad = out_grad.reshape(micro * tokens, features)
    new_rows = all_new.reshape(sections, fold, slots, width).transpose(0, 2, 1, 3).reshape(sections, slots, features)
    for layer in range(sections - 1, -1, -1):
        for slot in range(slots):
            in_grad = jnp.where(token == all_ids[layer, 0, slot], new_rows[layer, slot][None, :], in_grad)
    in_grad = in_grad.reshape(1, micro, tokens, features)
    return in_grad, grad_up.astype(jnp.bfloat16)[None], grad_down.astype(jnp.bfloat16)[None]


def solution(mesh):
    return jax.shard_map(
        functools.partial(per_device, mesh.shape["section"], mesh.shape["dp"]),
        mesh=mesh,
        in_specs=(
            P(None, "dp", None),
            P("section", None, None, None),
            P("section", None, None, "dp"),
            P("section", "dp", None),
            P("section", "dp", None),
            P("section", None, "dp"),
            P("section", None, "dp"),
            P("section", None, "dp"),
        ),
        out_specs=(
            P("section", None, "dp", None),
            P("section", "dp", None),
            P("section", "dp", None),
        ),
        check_vma=False,
    )
```

time: 343 us -> 112 us (0.33)
  matrix products: 162 us -> 11.4 us
  Pallas kernels: 0 us -> 73.6 us
  blocking collectives: 48.5 us -> 0 us
  waiting for transfers between devices: 37.9 us -> 0 us
  other arithmetic: 52.8 us -> 16.4 us
  starting transfers between devices: 23.7 us -> 0 us
  local copies, waits for them, and re-layouts: 15.8 us -> 9.16 us
    dot_general x20 -> x2, matrix products: 162 us -> 11.4 us  [the longest x1 5.69 us: per_device(): jnp.einsum('rh,rd->hd', hidden, x_rows[0].reshape(-1, features), preferre...]
    pallas_call x0 -> x1, Pallas kernels: none -> 73.6 us  [per_device(): pl.pallas_call(functools.partial(chain_kernel, (sections, peers, fold, sl...]
    all_gather x5 -> x0, blocking collectives: 48.5 us -> none  [tick_step(): row_piece = lax.all_gather(scaled, 'dp', axis=0, tiled=True)]
    ppermute x5 -> x0, waiting for transfers between devices: 37.6 us -> none  [from_behind(): return lax.ppermute(block, axis, route)]
    broadcast_in_dim x1 -> x0, other arithmetic: 17.7 us -> none  [per_device(): grad_down.astype(jnp.bfloat16)[None]]
    select_n x15 -> x3, other arithmetic: 21.2 us -> 3.75 us  [the longest x1 3.74 us: per_device(): jnp.where(token == all_ids[layer, 0, slot], new_rows[layer, slot][None, :...]
    all_to_all x5 -> x0, starting transfers between devices: 17.3 us -> none  [tick_step(): lax.all_to_all(partial_value, 'dp', split_axis=0, concat_axis=0, tiled=True)]
    eq x0 -> x8, other arithmetic: none -> 10.1 us  [per_device(): token == all_ids[layer, 0, slot]]
  transfers between devices with their start and end apart: 10 -> 0, of which waited for: 6 -> 0; matrix products, arithmetic and copies ran while one was open for 37% -> 0% of each run, Pallas kernels for 0% -> 0%
where the time goes in v1:
time: 112 us; the launch traced here: 111 us
  Pallas kernels  73.6 us (66%)
  other arithmetic  16.4 us (15%)
  matrix products  11.4 us (10%)
  local copies, waits for them, and re-layouts  9.16 us (8%)
    pallas_call x1, Pallas kernels, per_device(): pl.pallas_call(functools.partial(chain_kernel, (sections, peers, fold, sl...  73.6 us
    eq x8, other arithmetic, per_device(): token == all_ids[layer, 0, slot]  10.1 us
    dot_general x1, matrix products, per_device(): jnp.einsum('rh,rd->hd', hidden, x_rows[0].reshape(-1, features), preferre...  5.69 us
    dot_general x1, matrix products, per_device(): jnp.einsum('rh,rd->hd', activation, scaled, preferred_element_type=jnp.fl...  5.68 us
    select_n x1, other arithmetic, per_device(): jnp.where(token == all_ids[layer, 0, slot], new_rows[layer, slot][None, :...  3.74 us

profile of v1, /device:TPU:0, one launch (start us, length us, event | category | flops | bytes accessed | tf_op | source)
XLA Modules:
  0.0 111.4 jit_solution(8865259130061562374)
XLA Ops:
  0.6 0.0 copy-start
  0.6 1.0 copy-done
  1.6 0.8 squeeze.68
  2.4 0.7 iota_compare_fusion.1
  3.1 0.1 lt.51
  3.2 0.8 squeeze.69
  4.0 0.1 add.86
  4.1 0.1 add.87
  4.1 0.2 fusion.3
  4.3 0.1 tile.22
  4.4 0.1 broadcast_add_fusion
  4.5 0.1 add.91
  4.6 0.7 fusion.6
  5.3 0.1 reshape.475
  5.4 0.1 broadcast_in_dim.260
  5.5 0.1 broadcast_in_dim.263
  5.6 0.1 broadcast_in_dim.262.id_col_ref
  5.6 0.1 broadcast_in_dim.261.weight_ref
  5.7 1.6 %gather_fusion = bf16[4,6144]{1,0:T(4,128)(2,1)S(1)} fusion(bf16[2,64,6144]{2,1,0:T(8,128)(2,1)} %param.8, s32[4]{0:T(128)S(1)} %reshape.475), kind=kCustom, calls=%fused_computation | custom fusion | bytes 98336 | tf_op jit(solution)/shard_map/gather | solution.py:208
  7.3 0.8 multiply_convert_fusion
  8.1 0.8 copy.23
  9.1 0.1 broadcast_in_dim.268
  9.2 0.1 reshape.467.slope_ref
  9.3 73.6 %shard_map.103 = (bf16[4,16,1536]{2,1,0:T(8,128)(2,1)S(1)}, s32[4,8,128]{2,1,0:T(8,128)S(1)}, bf16[128,1536]{1,0:T(8,128)(2,1)S(1)}, bf16[128,672]{1,0:T(8,128)(2,1)S(1)}) custom-call(bf16[16,1536]{1,0:T(8,128)(2,1)S(1)} %reshape.466.base_ref, f32[16,128]{1,0:T(8,128)S(1)} %broadcast_in_dim.261.weight_ref, s32[16,128]{1,0:T(8,128)S(1)} %broadcast_in_dim.262.id_col_ref, ...), custom_call_target="tpu_custom_call" | custom-call | tf_op jit(solution)/shard_map/pallas_call | solution.py:229
  82.9 0.7 fusion.23
  83.6 1.3 %fusion.21 = (pred[2,64]{1,0:T(4,128)(4,1)S(1)}, pred[2,64]{1,0:T(4,128)(4,1)S(1)}) fusion(s32[]{:T(128)} %bitcast.12, s32[]{:T(128)} %bitcast.9), kind=kLoop, calls=%fused_computation.49 | loop fusion | flops 512 | bytes 264 | tf_op jit(solution)/shard_map/eq | solution.py:273
  84.9 1.3 %fusion.7 = (pred[2,64]{1,0:T(4,128)(4,1)S(1)}, pred[2,64]{1,0:T(4,128)(4,1)S(1)}) fusion(s32[]{:T(128)} %bitcast.27, s32[]{:T(128)} %bitcast.26), kind=kLoop, calls=%fused_computation.35 | loop fusion | flops 512 | bytes 264 | tf_op jit(solution)/shard_map/eq | solution.py:273
  86.2 1.3 %fusion.9 = (pred[2,64]{1,0:T(4,128)(4,1)S(1)}, pred[2,64]{1,0:T(4,128)(4,1)S(1)}) fusion(s32[]{:T(128)} %bitcast.25, s32[]{:T(128)} %bitcast.24), kind=kLoop, calls=%fused_computation.37 | loop fusion | flops 512 | bytes 264 | tf_op jit(solution)/shard_map/eq | solution.py:273
  87.5 1.3 %fusion.11 = (pred[2,64]{1,0:T(4,128)(4,1)S(1)}, pred[2,64]{1,0:T(4,128)(4,1)S(1)}) fusion(s32[]{:T(128)} %bitcast.23, s32[]{:T(128)} %bitcast.22), kind=kLoop, calls=%fused_computation.39 | loop fusion | flops 512 | bytes 264 | tf_op jit(solution)/shard_map/eq | solution.py:273
  88.7 1.2 %fusion.13 = (pred[2,64]{1,0:T(4,128)(4,1)S(1)}, pred[2,64]{1,0:T(4,128)(4,1)S(1)}) fusion(s32[]{:T(128)} %bitcast.21, s32[]{:T(128)} %bitcast.20), kind=kLoop, calls=%fused_computation.41 | loop fusion | flops 512 | bytes 264 | tf_op jit(solution)/shard_map/eq | solution.py:273
  90.0 1.3 %fusion.15 = (pred[2,64]{1,0:T(4,128)(4,1)S(1)}, pred[2,64]{1,0:T(4,128)(4,1)S(1)}) fusion(s32[]{:T(128)} %bitcast.19, s32[]{:T(128)} %bitcast.18), kind=kLoop, calls=%fused_computation.43 | loop fusion | flops 512 | bytes 264 | tf_op jit(solution)/shard_map/eq | solution.py:273
  91.2 1.2 %fusion.17 = (pred[2,64]{1,0:T(4,128)(4,1)S(1)}, pred[2,64]{1,0:T(4,128)(4,1)S(1)}) fusion(s32[]{:T(128)} %bitcast.17, s32[]{:T(128)} %bitcast.16), kind=kLoop, calls=%fused_computation.45 | loop fusion | flops 512 | bytes 264 | tf_op jit(solution)/shard_map/eq | solution.py:273
  92.5 1.3 %fusion.19 = (pred[2,64]{1,0:T(4,128)(4,1)S(1)}, pred[2,64]{1,0:T(4,128)(4,1)S(1)}) fusion(s32[]{:T(128)} %bitcast.15, s32[]{:T(128)} %bitcast.14), kind=kLoop, calls=%fused_computation.47 | loop fusion | flops 512 | bytes 264 | tf_op jit(solution)/shard_map/eq | solution.py:273
  93.8 0.1 reshape.468
  93.8 1.0 slice_reduce_fusion.15
  94.9 0.0 copy-start.1
  94.9 0.1 reshape.470
  95.1 0.1 reshape.472
  95.2 0.2 copy.28
  95.4 0.1 copy.29
  95.5 0.8 copy-done.1
  96.3 3.7 %select_bitcast_fusion = bf16[1,2,64,6144]{3,2,1,0:T(8,128)(2,1)} fusion(bf16[2,64,6144]{2,1,0:T(8,128)(2,1)S(1)} %copy-done.1, pred[2,64]{1,0:T(4,128)(4,1)S(1)} %get-tuple-element.43, pred[2,64]{1,0:T(4,128)(4,1)S(1)} %get-tuple-element.44, pred[2,64]{1,0:T(4,128)(4,1)S(1)} %get-tuple-element.45, pred[2,64]{1,0:T(4,128)(4,1)S(1)} %get-tuple-element.46, ...), kind=kLoop, calls=%fused_computation.5 | loop fusion | flops 12582912 | bytes 3344384 | tf_op jit(solution)/shard_map/jit(_where)/select_n | solution.py:273
  100.0 5.7 %fusion.1 = bf16[1,672,6144]{2,1,0:T(8,128)(2,1)} fusion(bf16[32,672]{1,0:T(8,128)(2,1)S(1)} %bitcast.61, bf16[32,6144]{1,0:T(8,128)(2,1)S(1)} %bitcast.57), kind=kOutput, calls=%fused_computation.4 | convolution fusion | flops 268369920 | bytes 8693760 | tf_op jit(solution)/shard_map/rh,rd->hd/dot_general | solution.py:264
  105.7 5.7 %fusion = bf16[1,672,6144]{2,1,0:T(8,128)(2,1)} fusion(bf16[32,672]{1,0:T(8,128)(2,1)S(1)} %reshape.471, bf16[32,6144]{1,0:T(8,128)(2,1)S(1)} %bitcast.53), kind=kOutput, calls=%fused_computation.3 | convolution fusion | flops 268369920 | bytes 8693760 | tf_op jit(solution)/shard_map/rh,rd->hd/dot_general | solution.py:265
  (17 shorter events, 0.3 us)
Async XLA Ops:
  0.6 1.0 copy-start
  94.9 1.4 %copy-start.1 = (bf16[2,64,6144]{2,1,0:T(8,128)(2,1)S(1)}, bf16[2,64,6144]{2,1,0:T(8,128)(2,1)}, u32[]{:S(2)}) copy-start(bf16[2,64,6144]{2,1,0:T(8,128)(2,1)} %param.8) | copy-start | bytes 4718596

commit v2 on v1

v2 whole, which is shorter than its diff:
```python
import functools

import jax
import jax.numpy as jnp
from jax import lax
from jax.experimental import pallas as pl
from jax.experimental.pallas import tpu as pltpu
from jax.sharding import PartitionSpec as P

MESH = pl.DeviceIdType.MESH
TILE_ROWS = 16
CHUNKS = 3


def row_of_slot(index, peers, cap, micro):
    slot = index % (micro * cap)
    return (slot // cap) * (peers * cap) + (index // TILE_ROWS) * cap + slot % cap


def chain_kernel(
    sizes,
    token_ref, gate_ref, count_ref, grad_ref, saved_ref, w_up_hbm, w_down_hbm,
    all_new_ref, all_ids_ref, gathered_ref, hidden_ref,
    w_up, w_down, gbuf, send_buf, recv_buf, new_buf, id_buf, cur_buf, slope_buf,
    weight_sem, gather_send, gather_recv, reduce_send, reduce_recv, id_send, id_recv, new_send, new_recv,
):
    sections, peers, micro, cap = sizes
    slots = micro * cap
    fold = TILE_ROWS // slots
    section = lax.axis_index("section")
    me = lax.axis_index("dp")
    width = gbuf.shape[1]
    c_width = width // CHUNKS
    hid = w_down.shape[0]
    tokens = grad_ref.shape[1]
    span = micro * tokens
    rows = peers * TILE_ROWS

    down_copy = pltpu.make_async_copy(w_down_hbm.at[0], w_down, weight_sem.at[0])
    up_copy = pltpu.make_async_copy(w_up_hbm.at[0], w_up, weight_sem.at[1])
    down_copy.start()
    up_copy.start()

    def peer_at(k):
        return lax.rem(me + k, peers)

    barrier = pltpu.get_barrier_semaphore()

    def greet(k, carry):
        pl.semaphore_signal(barrier, inc=1, device_id=(section, peer_at(k)), device_id_type=MESH)
        return carry

    lax.fori_loop(1, peers, greet, 0)
    for k in range(1, sections):
        other = lax.rem(section + k, sections)
        pl.semaphore_signal(barrier, inc=1, device_id=(other, me), device_id_type=MESH)

    flat, weight = [], []
    for m in range(micro):
        for c in range(cap):
            flat.append(token_ref[0, m, c] + m * tokens)
            weight.append(jnp.where(c < count_ref[0, m, 0], gate_ref[0, m, c], jnp.float32(0.0)))
    sent = []
    for k in range(slots):
        mine = flat[k]
        for e in range(k):
            mine = jnp.where(flat[e] == flat[k], -sections * TILE_ROWS * span, mine)
        sent.append(mine)

    def spread(values, slot, start):
        out = start
        for k in range(slots):
            out = jnp.where(slot == k, values[k], out)
        return out

    row = lax.broadcasted_iota(jnp.int32, (TILE_ROWS, 128), 0)
    lane = lax.broadcasted_iota(jnp.int32, (8, 128), 1)
    lane_all = lax.broadcasted_iota(jnp.int32, (8, rows), 1) % TILE_ROWS
    id_col = spread(flat, row % slots, jnp.zeros((TILE_ROWS, 128), jnp.int32)) + row // slots * span
    weight_col = spread(weight, row % slots, jnp.zeros((TILE_ROWS, 128), jnp.float32))
    id_row = spread(flat, lane_all % slots, jnp.zeros((8, rows), jnp.int32)) + lane_all // slots * span
    sent_row = spread(sent, lane % slots, jnp.zeros((8, 128), jnp.int32)) + lane // slots * span
    id_buf[section] = jnp.where((lane < TILE_ROWS) & (sent_row >= 0), sent_row, -1)

    flat_col = id_col[:, :1] % span
    piece_col = lax.broadcasted_iota(jnp.int32, (TILE_ROWS, span), 0) // slots
    token_lane = lax.broadcasted_iota(jnp.int32, (TILE_ROWS, span), 1)
    base = jnp.zeros((TILE_ROWS, width), jnp.float32)
    for piece in range(fold):
        pick = jnp.where((token_lane == flat_col) & (piece_col == piece), 1.0, 0.0).astype(jnp.bfloat16)
        part = grad_ref[:, :, piece * width:(piece + 1) * width].reshape(span, width)
        base = base + jnp.dot(pick, part, preferred_element_type=jnp.float32)
    cur_buf[...] = base

    source = row_of_slot(lax.broadcasted_iota(jnp.int32, (rows, slots * peers), 0), peers, cap, micro)
    order = jnp.where(source == lax.broadcasted_iota(jnp.int32, (rows, slots * peers), 1), 1.0, 0.0)
    pre = jnp.dot(order.astype(jnp.bfloat16), saved_ref[0].reshape(slots * peers, hid), preferred_element_type=jnp.float32)
    sigmoid = jax.nn.sigmoid(pre)
    slope_buf[...] = sigmoid * (1.0 + pre * (1.0 - sigmoid))

    pl.semaphore_wait(barrier, peers - 1 + sections - 1)

    def id_copy(source, target):
        return pltpu.make_async_remote_copy(
            src_ref=id_buf.at[source], dst_ref=id_buf.at[source],
            send_sem=id_send.at[target], recv_sem=id_recv.at[source],
            device_id=(target, me), device_id_type=MESH)

    def columns_of(chunk):
        return pl.ds(chunk * c_width, c_width)

    def rows_of(peer):
        return pl.ds(pl.multiple_of(peer * TILE_ROWS, TILE_ROWS), TILE_ROWS)

    def new_copy(chunk, source, target):
        place = new_buf.at[source, :, columns_of(chunk)]
        return pltpu.make_async_remote_copy(
            src_ref=place, dst_ref=place,
            send_sem=new_send.at[chunk, target], recv_sem=new_recv.at[chunk, source],
            device_id=(target, me), device_id_type=MESH)

    def gather_copy(chunk, source, target):
        place = gbuf.at[rows_of(source), columns_of(chunk)]
        return pltpu.make_async_remote_copy(
            src_ref=place, dst_ref=place,
            send_sem=gather_send.at[chunk, target], recv_sem=gather_recv.at[chunk, source],
            device_id=(section, target), device_id_type=MESH)

    def reduce_copy(chunk, source, target):
        return pltpu.make_async_remote_copy(
            src_ref=send_buf.at[rows_of(target), columns_of(chunk)],
            dst_ref=recv_buf.at[rows_of(source), columns_of(chunk)],
            send_sem=reduce_send.at[chunk, target], recv_sem=reduce_recv.at[chunk, source],
            device_id=(section, target), device_id_type=MESH)

    for target in range(sections - 1):
        @pl.when(target < section)
        def _():
            id_copy(section, target).start()

    def take_newer(upper, columns):
        picks = jnp.where(id_col[:, :TILE_ROWS] == id_buf[upper][:1, :TILE_ROWS], 1.0, 0.0)
        hit = jnp.max(picks, axis=1, keepdims=True) > 0.5
        taken = jnp.dot(picks.astype(jnp.bfloat16), new_buf[upper, :, columns], preferred_element_type=jnp.float32)
        cur_buf[:, columns] = jnp.where(hit, taken, cur_buf[:, columns])

    for upper in range(sections - 1, 1, -1):
        @pl.when(upper > section + 1)
        def _():
            id_copy(upper, upper).wait_recv()
            for chunk in range(CHUNKS):
                new_copy(chunk, upper, upper).wait_recv()
            take_newer(upper, slice(0, width))

    above = lax.rem(section + 1, sections)
    has_above = section < sections - 1

    @pl.when(has_above)
    def _():
        id_copy(above, above).wait_recv()

    my_rows = rows_of(me)
    for chunk in range(CHUNKS):
        columns = slice(chunk * c_width, (chunk + 1) * c_width)

        @pl.when(has_above)
        def _():
            new_copy(chunk, above, above).wait_recv()
            take_newer(above, columns)

        gbuf[my_rows, columns] = (weight_col[:, :1] * cur_buf[:, columns]).astype(jnp.bfloat16)

        def send(k, carry):
            gather_copy(chunk, me, peer_at(k)).start()
            return carry

        lax.fori_loop(1, peers, send, 0)

    down_copy.wait()
    row_piece = lax.broadcasted_iota(jnp.int32, (rows, c_width), 0) % TILE_ROWS // slots
    keep = [jnp.where(row_piece == piece, 1.0, 0.0).astype(jnp.bfloat16) for piece in range(fold)]
    total = jnp.zeros((hid, rows), jnp.float32)
    for chunk in range(CHUNKS):
        def arrive(k, carry):
            peer = peer_at(k)
            gather_copy(chunk, peer, peer).wait_recv()
            return carry

        lax.fori_loop(1, peers, arrive, 0)
        block = gbuf[:, chunk * c_width:(chunk + 1) * c_width]
        starts = [piece * width + chunk * c_width for piece in range(fold)]
        left = jnp.concatenate([w_down[:, start:start + c_width] for start in starts], axis=1)
        right = jnp.concatenate([block * keep[piece] for piece in range(fold)], axis=1)
        total = total + lax.dot_general(
            left, right, (((1,), (1,)), ((), ())), preferred_element_type=jnp.float32)

    back = total.T.reshape(peers, TILE_ROWS, hid)
    summed = back
    for k in range(1, fold):
        cut = k * slots
        summed = summed + jnp.concatenate([back[:, cut:], back[:, :cut]], axis=1)
    hidden = (summed.reshape(rows, hid) * slope_buf[...]).astype(jnp.bfloat16)

    up_copy.wait()
    for chunk in range(CHUNKS):
        partial = jnp.zeros((rows, c_width), jnp.float32)
        for piece in range(fold):
            start = piece * width + chunk * c_width
            product = jnp.dot(hidden, w_up[:, start:start + c_width], preferred_element_type=jnp.float32)
            partial = jnp.where(row_piece == piece, product, partial)
        columns = slice(chunk * c_width, (chunk + 1) * c_width)
        send_buf[:, columns] = partial.astype(jnp.bfloat16)

        def send(k, carry):
            reduce_copy(chunk, me, peer_at(k)).start()
            return carry

        lax.fori_loop(1, peers, send, 0)
        recv_buf[my_rows, columns] = send_buf[my_rows, columns]

    hidden_ref[...] = hidden
    gathered_ref[...] = gbuf[...]
    for layer in range(sections):
        @pl.when(layer > section)
        def _():
            all_new_ref[layer] = new_buf[layer]
            all_ids_ref[layer] = id_buf[layer]

        @pl.when(layer < section)
        def _():
            all_new_ref[layer] = jnp.zeros((TILE_ROWS, width), jnp.bfloat16)
            all_ids_ref[layer] = jnp.full((8, 128), -1, jnp.int32)
    all_ids_ref[section] = id_buf[section]

    alike = jnp.where(id_col[:, :1] == id_row[:1, :], 1.0, 0.0).astype(jnp.bfloat16)
    for chunk in range(CHUNKS):
        def arrive(k, carry):
            peer = peer_at(k)
            reduce_copy(chunk, peer, peer).wait_recv()
            return carry

        lax.fori_loop(1, peers, arrive, 0)
        columns = slice(chunk * c_width, (chunk + 1) * c_width)
        delta = jnp.dot(alike, recv_buf[:, columns], preferred_element_type=jnp.float32)
        new_buf[section, :, columns] = (cur_buf[:, columns] + delta).astype(jnp.bfloat16)

        @pl.when(section > 0)
        def _():
            new_copy(chunk, section, section - 1).start()

    for target in range(sections - 2):
        @pl.when(target < section - 1)
        def _():
            for chunk in range(CHUNKS):
                new_copy(chunk, section, target).start()
    all_new_ref[section] = new_buf[section]

    def drain(k, carry):
        peer = peer_at(k)
        for chunk in range(CHUNKS):
            gather_copy(chunk, me, peer).wait_send()
            reduce_copy(chunk, me, peer).wait_send()
        return carry

    lax.fori_loop(1, peers, drain, 0)
    for target in range(sections - 1):
        @pl.when(target < section)
        def _():
            id_copy(section, target).wait_send()
            for chunk in range(CHUNKS):
                new_copy(chunk, section, target).wait_send()


def gradient_kernel(
    sizes,
    hidden_ref, gathered_ref, saved_ref, x_ref, grad_ref, new_ref, id_ref,
    in_grad_ref, grad_up_ref, grad_down_ref,
    hidden_t, activation_t, picks, order_buf,
):
    sections, peers, micro, cap, per_piece = sizes
    slots = micro * cap
    step = pl.program_id(0)
    piece = step // per_piece
    hid = hidden_t.shape[0]
    all_slots = peers * slots
    rows = peers * TILE_ROWS
    span = grad_ref.shape[0] * grad_ref.shape[1]
    index = lax.broadcasted_iota(jnp.int32, (all_slots, rows), 1)

    @pl.when(step == 0)
    def _():
        place = row_of_slot(index, peers, cap, micro)
        order = jnp.where(place == lax.broadcasted_iota(jnp.int32, (all_slots, rows), 0), 1.0, 0.0)
        order_buf[...] = order
        first = jnp.where(index % TILE_ROWS < slots, order, 0.0).astype(jnp.bfloat16)
        hidden = jnp.dot(first, hidden_ref[...], preferred_element_type=jnp.float32)
        hidden_t[...] = hidden.T.astype(jnp.bfloat16)
        pre = saved_ref[0].reshape(all_slots, hid).astype(jnp.float32)
        activation_t[...] = (pre * jax.nn.sigmoid(pre)).T.astype(jnp.bfloat16)
        token = lax.broadcasted_iota(jnp.int32, (span, TILE_ROWS), 0)
        found = jnp.zeros((span, 1), jnp.float32)
        for layer in range(sections):
            ids = id_ref[layer][:1, :TILE_ROWS]
            same = jnp.where((token == ids % span) & (ids >= 0), 1.0, 0.0) * (1.0 - found)
            picks[:, layer * TILE_ROWS:(layer + 1) * TILE_ROWS] = same
            found = jnp.maximum(found, jnp.max(same, axis=1, keepdims=True))

    width = x_ref.shape[3]
    mine = jnp.where(index % TILE_ROWS // slots == piece, order_buf[...], 0.0).astype(jnp.bfloat16)
    scaled = jnp.dot(mine, gathered_ref[...], preferred_element_type=jnp.float32).astype(jnp.bfloat16)
    grad_down_ref[0] = jnp.dot(
        activation_t[...], scaled, preferred_element_type=jnp.float32).astype(jnp.bfloat16)
    grad_up_ref[0] = jnp.dot(
        hidden_t[...], x_ref[0].reshape(all_slots, width), preferred_element_type=jnp.float32).astype(jnp.bfloat16)

    lane = lax.broadcasted_iota(jnp.int32, picks.shape, 1)
    chosen = jnp.where(lane % TILE_ROWS // slots == piece, picks[...], 0.0)
    hit = jnp.max(chosen, axis=1, keepdims=True) > 0.5
    newest = jnp.dot(
        chosen.astype(jnp.bfloat16), new_ref[...].reshape(sections * TILE_ROWS, width),
        preferred_element_type=jnp.float32)
    old = grad_ref[...].reshape(span, width).astype(jnp.float32)
    in_grad_ref[0] = jnp.where(hit, newest, old).astype(jnp.bfloat16).reshape(grad_ref.shape)


def per_device(sections, peers, out_grad, x_rows, saved_u, w_up_t, w_down, gate, route_tokens, route_count):
    micro, tokens, features = out_grad.shape
    cap = gate.shape[2]
    slots = micro * cap
    fold = TILE_ROWS // slots
    width = features // fold
    hid = w_down.shape[1]
    rows = peers * TILE_ROWS
    sizes = (sections, peers, micro, cap)

    vmem = pl.BlockSpec(memory_space=pltpu.VMEM)
    smem = pl.BlockSpec(memory_space=pltpu.SMEM)
    hbm = pl.BlockSpec(memory_space=pl.ANY)
    dma = pltpu.SemaphoreType.DMA
    all_new, all_ids, gathered, hidden = pl.pallas_call(
        functools.partial(chain_kernel, sizes),
        out_shape=(
            jax.ShapeDtypeStruct((sections, TILE_ROWS, width), jnp.bfloat16),
            jax.ShapeDtypeStruct((sections, 8, 128), jnp.int32),
            jax.ShapeDtypeStruct((rows, width), jnp.bfloat16),
            jax.ShapeDtypeStruct((rows, hid), jnp.bfloat16),
        ),
        in_specs=[smem, smem, smem, vmem, vmem, hbm, hbm],
        out_specs=(vmem,) * 4,
        scratch_shapes=[
            pltpu.VMEM((hid, features), jnp.bfloat16),
            pltpu.VMEM((hid, features), jnp.bfloat16),
            pltpu.VMEM((rows, width), jnp.bfloat16),
            pltpu.VMEM((rows, width), jnp.bfloat16),
            pltpu.VMEM((rows, width), jnp.bfloat16),
            pltpu.VMEM((sections, TILE_ROWS, width), jnp.bfloat16),
            pltpu.VMEM((sections, 8, 128), jnp.int32),
            pltpu.VMEM((TILE_ROWS, width), jnp.float32),
            pltpu.VMEM((rows, hid), jnp.float32),
            dma((2,)),
            dma((CHUNKS, peers)),
            dma((CHUNKS, peers)),
            dma((CHUNKS, peers)),
            dma((CHUNKS, peers)),
            dma((sections,)),
            dma((sections,)),
            dma((CHUNKS, sections)),
            dma((CHUNKS, sections)),
        ],
        compiler_params=pltpu.CompilerParams(
            collective_id=0, has_side_effects=True, vmem_limit_bytes=48 * 1024 * 1024),
    )(route_tokens, gate, route_count, out_grad, saved_u, w_up_t, w_down)

    per_piece = CHUNKS
    block = width // per_piece
    slot_rows = peers * cap
    return pl.pallas_call(
        functools.partial(gradient_kernel, sizes + (per_piece,)),
        grid=(fold * per_piece,),
        out_shape=(
            jax.ShapeDtypeStruct((1, micro, tokens, features), jnp.bfloat16),
            jax.ShapeDtypeStruct((1, hid, features), jnp.bfloat16),
            jax.ShapeDtypeStruct((1, hid, features), jnp.bfloat16),
        ),
        in_specs=[
            pl.BlockSpec((rows, hid), lambda i: (0, 0)),
            pl.BlockSpec((rows, block), lambda i: (0, i % per_piece)),
            pl.BlockSpec((1, micro, slot_rows, hid), lambda i: (0, 0, 0, 0)),
            pl.BlockSpec((1, micro, slot_rows, block), lambda i: (0, 0, 0, i)),
            pl.BlockSpec((micro, tokens, block), lambda i: (0, 0, i)),
            pl.BlockSpec((sections, TILE_ROWS, block), lambda i: (0, 0, i % per_piece)),
            pl.BlockSpec((sections, 8, 128), lambda i: (0, 0, 0)),
        ],
        out_specs=(
            pl.BlockSpec((1, micro, tokens, block), lambda i: (0, 0, 0, i)),
            pl.BlockSpec((1, hid, block), lambda i: (0, 0, i)),
            pl.BlockSpec((1, hid, block), lambda i: (0, 0, i)),
        ),
        scratch_shapes=[
            pltpu.VMEM((hid, peers * slots), jnp.bfloat16),
            pltpu.VMEM((hid, peers * slots), jnp.bfloat16),
            pltpu.VMEM((micro * tokens, sections * TILE_ROWS), jnp.float32),
            pltpu.VMEM((peers * slots, rows), jnp.float32),
        ],
        compiler_params=pltpu.CompilerParams(vmem_limit_bytes=32 * 1024 * 1024),
    )(hidden, gathered, saved_u, x_rows, out_grad, all_new, all_ids)


def solution(mesh):
    return jax.shard_map(
        functools.partial(per_device, mesh.shape["section"], mesh.shape["dp"]),
        mesh=mesh,
        in_specs=(
            P(None, "dp", None),
            P("section", None, None, None),
            P("section", None, None, "dp"),
            P("section", "dp", None),
            P("section", "dp", None),
            P("section", None, "dp"),
            P("section", None, "dp"),
            P("section", None, "dp"),
        ),
        out_specs=(
            P("section", None, "dp", None),
            P("section", "dp", None),
            P("section", "dp", None),
        ),
        check_vma=False,
    )
```

time: 112 us -> 91.2 us (0.81)
  other arithmetic: 16.4 us -> 0 us
  Pallas kernels: 73.6 us -> 86 us
  matrix products: 11.4 us -> 0 us
  local copies, waits for them, and re-layouts: 9.16 us -> 4.31 us
    pallas_call x1 -> x2, Pallas kernels: 73.6 us -> 86 us  [the longest x1 74.2 us: per_device(): pl.pallas_call(functools.partial(chain_kernel, sizes), out_shape=(jax.Sha...]
    dot_general x2 -> x0, matrix products: 11.4 us -> none  [the longest x1 5.69 us: per_device(): jnp.einsum('rh,rd->hd', hidden, x_rows[0].reshape(-1, features), preferre...]
    eq x8 -> x0, other arithmetic: 10.1 us -> none  [per_device(): token == all_ids[layer, 0, slot]]
    select_n x3 -> x0, other arithmetic: 3.75 us -> none  [the longest x1 3.74 us: per_device(): jnp.where(token == all_ids[layer, 0, slot], new_rows[layer, slot][None, :...]
    unnamed x5 -> x11, local copies, waits for them, and re-layouts: 1.85 us -> 4.31 us
    slice x2 -> x0, local copies, waits for them, and re-layouts: 1.74 us -> none  [the longest x1 1.03 us: per_device(): new_rows[layer, slot][None, :]]
    gather x1 -> x0, local copies, waits for them, and re-layouts: 1.59 us -> none  [per_device(): out_grad[jnp.arange(micro)[:, None], token_ids].reshape(slots, fold, width)]
    squeeze x2 -> x0, local copies, waits for them, and re-layouts: 1.52 us -> none  [the longest x1 0.76 us: per_device(): weights = jnp.where(live, gate[0], jnp.float32(0.0)).reshape(slots)]
where the time goes in v2:
time: 91.2 us; the launch traced here: 91 us
  Pallas kernels  86 us (94%)
  local copies, waits for them, and re-layouts  4.31 us (5%)
    pallas_call x1, Pallas kernels, per_device(): pl.pallas_call(functools.partial(chain_kernel, sizes), out_shape=(jax.Sha...  74.2 us
    pallas_call x1, Pallas kernels, per_device(): pl.pallas_call(functools.partial(gradient_kernel, sizes + (per_piece,)),...  11.8 us
    unnamed x11, local copies, waits for them, and re-layouts  4.31 us

profile of v2, /device:TPU:0, one launch (start us, length us, event | category | flops | bytes accessed | tf_op | source)
XLA Modules:
  0.0 91.0 jit_solution(5998175102871174484)
XLA Ops:
  0.6 0.7 copy.11.count_ref
  1.4 0.0 copy-start
  1.4 1.4 %copy-done = bf16[2,64,6144]{2,1,0:T(8,128)(2,1)S(1)} copy-done((bf16[2,64,6144]{2,1,0:T(8,128)(2,1)S(1)}, bf16[2,64,6144]{2,1,0:T(8,128)(2,1)}, u32[]{:S(2)}) %copy-start) | copy-done | bytes 1572888
  2.8 0.0 copy-start.2
  2.8 0.8 copy-done.2
  3.6 0.0 copy-start.3
  3.6 0.7 copy-done.3
  4.3 0.0 copy-start.4
  4.3 0.7 copy-done.4
  4.9 0.0 copy-start.1
  4.9 74.2 %shard_map.103 = (bf16[4,16,1536]{2,1,0:T(8,128)(2,1)S(1)}, s32[4,8,128]{2,1,0:T(8,128)S(1)}, bf16[128,1536]{1,0:T(8,128)(2,1)S(1)}, bf16[128,672]{1,0:T(8,128)(2,1)S(1)}) custom-call(s32[1,2,2]{2,1,0:T(2,128)S(1)} %copy-done.3, f32[1,2,2]{2,1,0:T(2,128)S(1)} %copy-done.4, s32[1,2,1]{2,1,0:T(2,128)S(1)} %copy.11.count_ref, bf16[2,64,6144]{2,1,0:T(8,128)(2,1)S(1)} %copy-done, ...), custom_call_target="tpu_custom_call" | custom-call | tf_op jit(solution)/shard_map/pallas_call | solution.py:340
  79.2 0.0 copy-done.1
  79.2 11.8 %shard_map.104 = (bf16[1,2,64,6144]{3,2,1,0:T(8,128)(2,1)}, bf16[1,672,6144]{2,1,0:T(8,128)(2,1)}, bf16[1,672,6144]{2,1,0:T(8,128)(2,1)}) custom-call(bf16[128,672]{1,0:T(8,128)(2,1)S(1)} %get-tuple-element.7.hidden_ref, bf16[128,1536]{1,0:T(8,128)(2,1)S(1)} %get-tuple-element.8.gathered_ref, bf16[1,2,16,672]{3,2,1,0:T(8,128)(2,1)S(1)} %copy-done.2, ...), custom_call_target="tpu_custom_call" | custom-call | tf_op jit(solution)/shard_map/pallas_call | solution.py:377
Async XLA Ops:
  1.4 1.4 %copy-start = (bf16[2,64,6144]{2,1,0:T(8,128)(2,1)S(1)}, bf16[2,64,6144]{2,1,0:T(8,128)(2,1)}, u32[]{:S(2)}) copy-start(bf16[2,64,6144]{2,1,0:T(8,128)(2,1)} %grad_ref.3) | copy-start | bytes 4718596
  2.8 0.8 copy-start.2
  3.6 0.7 copy-start.3
  4.3 0.7 copy-start.4
  4.9 74.2 %copy-start.1 = (bf16[1,2,16,6144]{3,2,1,0:T(8,128)(2,1)S(1)}, bf16[1,2,16,6144]{3,2,1,0:T(8,128)(2,1)}, u32[]{:S(2)}) copy-start(bf16[1,2,16,6144]{3,2,1,0:T(8,128)(2,1)} %x_ref.1) | copy-start | bytes 1179652

commit v3 on v2

v3 whole, which is shorter than its diff:
```python
import functools

import jax
import jax.numpy as jnp
from jax import lax
from jax.experimental import pallas as pl
from jax.experimental.pallas import tpu as pltpu
from jax.sharding import PartitionSpec as P

MESH = pl.DeviceIdType.MESH
TILE_ROWS = 16
CHUNKS = 3


def row_of_slot(index, peers, cap, micro):
    slot = index % (micro * cap)
    block = index // TILE_ROWS
    peer = block % (peers // 2) * 2 + block // (peers // 2)
    return (slot // cap) * (peers * cap) + peer * cap + slot % cap


def chain_kernel(
    sizes,
    token_hbm, gate_hbm, count_hbm, grad_hbm, saved_hbm, w_up_hbm, w_down_hbm,
    all_new_ref, picks_ref, scaled_ref, hidden_t_ref, activation_t_ref,
    token_ref, gate_ref, count_ref, grad_ref, saved_ref,
    w_up, w_down, gbuf, send_buf, pair_buf, sum_buf, recv_buf, new_buf, id_buf, cur_buf, slope_buf,
    load_sem, gather_send, gather_recv, share_send, share_recv, pair_send, pair_recv,
    reduce_send, reduce_recv, id_send, id_recv, new_send, new_recv,
):
    sections, peers, micro, cap = sizes
    slots = micro * cap
    fold = TILE_ROWS // slots
    section = lax.axis_index("section")
    me = lax.axis_index("dp")
    width = gbuf.shape[1]
    c_width = width // CHUNKS
    hid = w_down.shape[0]
    tokens = grad_ref.shape[1]
    span = micro * tokens
    rows = peers * TILE_ROWS
    chips = peers // 2
    half = chips * TILE_ROWS
    core = lax.rem(me, 2)
    chip = me // 2
    sibling = me + 1 - 2 * core

    small = [
        pltpu.make_async_copy(source, target, load_sem.at[2 + k])
        for k, (source, target) in enumerate((
            (token_hbm, token_ref), (gate_hbm, gate_ref), (count_hbm, count_ref),
            (grad_hbm, grad_ref), (saved_hbm, saved_ref)))
    ]
    for copy in small:
        copy.start()
    down_copy = pltpu.make_async_copy(w_down_hbm.at[0], w_down, load_sem.at[0])
    up_copy = pltpu.make_async_copy(w_up_hbm.at[0], w_up, load_sem.at[1])
    down_copy.start()

    def chip_at(k):
        return lax.rem(chip + k, chips)

    barrier = pltpu.get_barrier_semaphore()

    def greet(k, carry):
        pl.semaphore_signal(barrier, inc=1, device_id=(section, chip_at(k) * 2 + core), device_id_type=MESH)
        return carry

    lax.fori_loop(1, chips, greet, 0)
    pl.semaphore_signal(barrier, inc=1, device_id=(section, sibling), device_id_type=MESH)
    for k in range(1, sections):
        other = lax.rem(section + k, sections)
        pl.semaphore_signal(barrier, inc=1, device_id=(other, me), device_id_type=MESH)

    for copy in small:
        copy.wait()

    flat, weight = [], []
    for m in range(micro):
        for c in range(cap):
            flat.append(token_ref[0, m, c] + m * tokens)
            weight.append(jnp.where(c < count_ref[0, m, 0], gate_ref[0, m, c], jnp.float32(0.0)))
    sent = []
    for k in range(slots):
        mine = flat[k]
        for e in range(k):
            mine = jnp.where(flat[e] == flat[k], -sections * TILE_ROWS * span, mine)
        sent.append(mine)

    def spread(values, slot, start):
        out = start
        for k in range(slots):
            out = jnp.where(slot == k, values[k], out)
        return out

    row = lax.broadcasted_iota(jnp.int32, (TILE_ROWS, 128), 0)
    lane = lax.broadcasted_iota(jnp.int32, (8, 128), 1)
    lane_all = lax.broadcasted_iota(jnp.int32, (8, half), 1) % TILE_ROWS
    id_col = spread(flat, row % slots, jnp.zeros((TILE_ROWS, 128), jnp.int32)) + row // slots * span
    weight_col = spread(weight, row % slots, jnp.zeros((TILE_ROWS, 128), jnp.float32))
    id_row = spread(flat, lane_all % slots, jnp.zeros((8, half), jnp.int32)) + lane_all // slots * span
    sent_row = spread(sent, lane % slots, jnp.zeros((8, 128), jnp.int32)) + lane // slots * span
    id_buf[section] = jnp.where((lane < TILE_ROWS) & (sent_row >= 0), sent_row, -1)

    flat_col = id_col[:, :1] % span
    piece_col = lax.broadcasted_iota(jnp.int32, (TILE_ROWS, span), 0) // slots
    token_lane = lax.broadcasted_iota(jnp.int32, (TILE_ROWS, span), 1)
    base = jnp.zeros((TILE_ROWS, width), jnp.float32)
    for piece in range(fold):
        pick = jnp.where((token_lane == flat_col) & (piece_col == piece), 1.0, 0.0).astype(jnp.bfloat16)
        part = grad_ref[:, :, piece * width:(piece + 1) * width].reshape(span, width)
        base = base + jnp.dot(pick, part, preferred_element_type=jnp.float32)
    cur_buf[...] = base

    pl.semaphore_wait(barrier, chips + sections - 1)

    def id_copy(source, target):
        return pltpu.make_async_remote_copy(
            src_ref=id_buf.at[source], dst_ref=id_buf.at[source],
            send_sem=id_send.at[target], recv_sem=id_recv.at[source],
            device_id=(target, me), device_id_type=MESH)

    def columns_of(chunk):
        return pl.ds(chunk * c_width, c_width)

    def rows_of(peer):
        return pl.ds(pl.multiple_of(peer * TILE_ROWS, TILE_ROWS), TILE_ROWS)

    def new_copy(chunk, source, target):
        place = new_buf.at[source, :, columns_of(chunk)]
        return pltpu.make_async_remote_copy(
            src_ref=place, dst_ref=place,
            send_sem=new_send.at[chunk, target], recv_sem=new_recv.at[chunk, source],
            device_id=(target, me), device_id_type=MESH)

    def block_of(a_chip, a_core):
        return pl.ds(pl.multiple_of(a_core * half + a_chip * TILE_ROWS, TILE_ROWS), TILE_ROWS)

    def half_of(a_core):
        return pl.ds(pl.multiple_of(a_core * half, TILE_ROWS), half)

    def gather_copy(chunk, source, target):
        place = gbuf.at[block_of(source, core), columns_of(chunk)]
        return pltpu.make_async_remote_copy(
            src_ref=place, dst_ref=place,
            send_sem=gather_send.at[chunk, target], recv_sem=gather_recv.at[chunk, source],
            device_id=(section, target * 2 + core), device_id_type=MESH)

    def share_copy(chunk, a_core):
        place = gbuf.at[half_of(a_core), columns_of(chunk)]
        return pltpu.make_async_remote_copy(
            src_ref=place, dst_ref=place,
            send_sem=share_send.at[chunk], recv_sem=share_recv.at[chunk],
            device_id=(section, sibling), device_id_type=MESH)

    def pair_copy(chunk):
        return pltpu.make_async_remote_copy(
            src_ref=send_buf.at[half_of(1 - core), columns_of(chunk)],
            dst_ref=pair_buf.at[:, columns_of(chunk)],
            send_sem=pair_send.at[chunk], recv_sem=pair_recv.at[chunk],
            device_id=(section, sibling), device_id_type=MESH)

    def reduce_copy(chunk, source, target):
        return pltpu.make_async_remote_copy(
            src_ref=sum_buf.at[rows_of(target), columns_of(chunk)],
            dst_ref=recv_buf.at[rows_of(source), columns_of(chunk)],
            send_sem=reduce_send.at[chunk, target], recv_sem=reduce_recv.at[chunk, source],
            device_id=(section, target * 2 + core), device_id_type=MESH)

    for target in range(sections - 1):
        @pl.when(target < section)
        def _():
            id_copy(section, target).start()

    def take_newer(upper, columns):
        picks = jnp.where(id_col[:, :TILE_ROWS] == id_buf[upper][:1, :TILE_ROWS], 1.0, 0.0)
        hit = jnp.max(picks, axis=1, keepdims=True) > 0.5
        taken = jnp.dot(picks.astype(jnp.bfloat16), new_buf[upper, :, columns], preferred_element_type=jnp.float32)
        cur_buf[:, columns] = jnp.where(hit, taken, cur_buf[:, columns])

    for upper in range(sections - 1, 1, -1):
        @pl.when(upper > section + 1)
        def _():
            id_copy(upper, upper).wait_recv()
            for chunk in range(CHUNKS):
                new_copy(chunk, upper, upper).wait_recv()
            take_newer(upper, slice(0, width))

    above = lax.rem(section + 1, sections)
    has_above = section < sections - 1

    def prepare():
        for layer in range(sections):
            @pl.when(layer < section)
            def _():
                all_new_ref[layer] = jnp.zeros((TILE_ROWS, width), jnp.bfloat16)
                id_buf[layer] = jnp.full((8, 128), -1, jnp.int32)
        pre = saved_ref[0].reshape(slots * peers, hid).astype(jnp.float32)
        activation_t_ref[...] = (pre * jax.nn.sigmoid(pre)).T.astype(jnp.bfloat16)
        token = lax.broadcasted_iota(jnp.int32, (span, TILE_ROWS), 0)
        found = jnp.zeros((span, 1), jnp.float32)
        for layer in range(sections):
            ids = id_buf[layer][:1, :TILE_ROWS]
            same = jnp.where((token == ids % span) & (ids >= 0), 1.0, 0.0) * (1.0 - found)
            picks_ref[:, layer * TILE_ROWS:(layer + 1) * TILE_ROWS] = same
            found = jnp.maximum(found, jnp.max(same, axis=1, keepdims=True))

    @pl.when(has_above)
    def _():
        id_copy(above, above).wait_recv()
        prepare()

    my_rows = block_of(chip, core)
    for chunk in range(CHUNKS):
        columns = slice(chunk * c_width, (chunk + 1) * c_width)

        @pl.when(has_above)
        def _():
            new_copy(chunk, above, above).wait_recv()
            take_newer(above, columns)

        gbuf[my_rows, columns] = (weight_col[:, :1] * cur_buf[:, columns]).astype(jnp.bfloat16)

        def send(k, carry):
            gather_copy(chunk, chip, chip_at(k)).start()
            return carry

        lax.fori_loop(1, chips, send, 0)

    source = row_of_slot(lax.broadcasted_iota(jnp.int32, (rows, slots * peers), 0), peers, cap, micro)
    order = jnp.where(source == lax.broadcasted_iota(jnp.int32, (rows, slots * peers), 1), 1.0, 0.0)
    pre = jnp.dot(order.astype(jnp.bfloat16), saved_ref[0].reshape(slots * peers, hid), preferred_element_type=jnp.float32)
    sigmoid = jax.nn.sigmoid(pre)
    slope_buf[...] = sigmoid * (1.0 + pre * (1.0 - sigmoid))

    down_copy.wait()
    up_copy.start()
    row_piece = lax.broadcasted_iota(jnp.int32, (rows, c_width), 0) % TILE_ROWS // slots
    keep = [jnp.where(row_piece == piece, 1.0, 0.0).astype(jnp.bfloat16) for piece in range(fold)]
    total = jnp.zeros((hid, rows), jnp.float32)
    def pass_on(chunk):
        def arrive(k, carry):
            other = chip_at(k)
            gather_copy(chunk, other, other).wait_recv()
            return carry

        lax.fori_loop(1, chips, arrive, 0)
        share_copy(chunk, core).start()

    pass_on(0)
    for chunk in range(CHUNKS):
        if chunk + 1 < CHUNKS:
            pass_on(chunk + 1)
        share_copy(chunk, 1 - core).wait_recv()
        block = gbuf[:, chunk * c_width:(chunk + 1) * c_width]
        starts = [piece * width + chunk * c_width for piece in range(fold)]
        left = jnp.concatenate([w_down[:, start:start + c_width] for start in starts], axis=1)
        right = jnp.concatenate([block * keep[piece] for piece in range(fold)], axis=1)
        total = total + lax.dot_general(
            left, right, (((1,), (1,)), ((), ())), preferred_element_type=jnp.float32)

    back = total.T.reshape(peers, TILE_ROWS, hid)
    summed = back
    for k in range(1, fold):
        cut = k * slots
        summed = summed + jnp.concatenate([back[:, cut:], back[:, :cut]], axis=1)
    hidden = (summed.reshape(rows, hid) * slope_buf[...]).astype(jnp.bfloat16)

    def send_sums(chunk):
        columns = slice(chunk * c_width, (chunk + 1) * c_width)
        pair_copy(chunk).wait_recv()
        both = send_buf[half_of(core), columns].astype(jnp.float32) + pair_buf[:, columns].astype(jnp.float32)
        sum_buf[:, columns] = both.astype(jnp.bfloat16)

        def send(k, carry):
            reduce_copy(chunk, chip, chip_at(k)).start()
            return carry

        lax.fori_loop(1, chips, send, 0)
        recv_buf[rows_of(chip), columns] = sum_buf[rows_of(chip), columns]

    up_copy.wait()
    for chunk in range(CHUNKS):
        partial = jnp.zeros((rows, c_width), jnp.float32)
        for piece in range(fold):
            start = piece * width + chunk * c_width
            product = jnp.dot(hidden, w_up[:, start:start + c_width], preferred_element_type=jnp.float32)
            partial = jnp.where(row_piece == piece, product, partial)
        columns = slice(chunk * c_width, (chunk + 1) * c_width)
        send_buf[:, columns] = partial.astype(jnp.bfloat16)

        pair_copy(chunk).start()
        if chunk > 0:
            send_sums(chunk - 1)
    send_sums(CHUNKS - 1)

    source = row_of_slot(lax.broadcasted_iota(jnp.int32, (slots * peers, rows), 1), peers, cap, micro)
    order = jnp.where(source == lax.broadcasted_iota(jnp.int32, (slots * peers, rows), 0), 1.0, 0.0)
    piece_lane = lax.broadcasted_iota(jnp.int32, (slots * peers, rows), 1) % TILE_ROWS // slots
    for piece in range(fold):
        mine = jnp.where(piece_lane == piece, order, 0.0).astype(jnp.bfloat16)
        if piece == 0:
            hidden_t_ref[...] = jnp.dot(mine, hidden, preferred_element_type=jnp.float32).T.astype(jnp.bfloat16)
        scaled_ref[:, piece * width:(piece + 1) * width] = jnp.dot(
            mine, gbuf[...], preferred_element_type=jnp.float32).astype(jnp.bfloat16)
    for layer in range(sections):
        @pl.when(layer > section)
        def _():
            all_new_ref[layer] = new_buf[layer]

    alike = jnp.where(id_col[:, :1] == id_row[:1, :], 1.0, 0.0).astype(jnp.bfloat16)
    for chunk in range(CHUNKS):
        def arrive(k, carry):
            other = chip_at(k)
            reduce_copy(chunk, other, other).wait_recv()
            return carry

        lax.fori_loop(1, chips, arrive, 0)
        columns = slice(chunk * c_width, (chunk + 1) * c_width)
        delta = jnp.dot(alike, recv_buf[:, columns], preferred_element_type=jnp.float32)
        new_buf[section, :, columns] = (cur_buf[:, columns] + delta).astype(jnp.bfloat16)

        @pl.when(section > 0)
        def _():
            new_copy(chunk, section, section - 1).start()

    for target in range(sections - 2):
        @pl.when(target < section - 1)
        def _():
            for chunk in range(CHUNKS):
                new_copy(chunk, section, target).start()
    all_new_ref[section] = new_buf[section]

    @pl.when(jnp.logical_not(has_above))
    def _():
        prepare()

    def drain(k, carry):
        other = chip_at(k)
        for chunk in range(CHUNKS):
            gather_copy(chunk, chip, other).wait_send()
            reduce_copy(chunk, chip, other).wait_send()
        return carry

    lax.fori_loop(1, chips, drain, 0)
    for chunk in range(CHUNKS):
        share_copy(chunk, core).wait_send()
        pair_copy(chunk).wait_send()
    for target in range(sections - 1):
        @pl.when(target < section)
        def _():
            id_copy(section, target).wait_send()
            for chunk in range(CHUNKS):
                new_copy(chunk, section, target).wait_send()


def gradient_kernel(
    sizes,
    hidden_t_ref, activation_t_ref, scaled_ref, x_ref, grad_ref, new_ref, picks_ref,
    in_grad_ref, grad_up_ref, grad_down_ref,
):
    sections, slots, per_piece = sizes
    piece = pl.program_id(0) // per_piece
    span = grad_ref.shape[0] * grad_ref.shape[1]
    width = x_ref.shape[3]
    grad_down_ref[0] = jnp.dot(
        activation_t_ref[...], scaled_ref[...], preferred_element_type=jnp.float32).astype(jnp.bfloat16)
    grad_up_ref[0] = jnp.dot(
        hidden_t_ref[...], x_ref[0].reshape(-1, width), preferred_element_type=jnp.float32).astype(jnp.bfloat16)

    lane = lax.broadcasted_iota(jnp.int32, picks_ref.shape, 1)
    chosen = jnp.where(lane % TILE_ROWS // slots == piece, picks_ref[...], 0.0)
    hit = jnp.max(chosen, axis=1, keepdims=True) > 0.5
    newest = jnp.dot(
        chosen.astype(jnp.bfloat16), new_ref[...].reshape(sections * TILE_ROWS, width),
        preferred_element_type=jnp.float32)
    old = grad_ref[...].reshape(span, width).astype(jnp.float32)
    in_grad_ref[0] = jnp.where(hit, newest, old).astype(jnp.bfloat16).reshape(grad_ref.shape)


def per_device(sections, peers, out_grad, x_rows, saved_u, w_up_t, w_down, gate, route_tokens, route_count):
    micro, tokens, features = out_grad.shape
    cap = gate.shape[2]
    slots = micro * cap
    fold = TILE_ROWS // slots
    width = features // fold
    hid = w_down.shape[1]
    rows = peers * TILE_ROWS
    sizes = (sections, peers, micro, cap)

    vmem = pl.BlockSpec(memory_space=pltpu.VMEM)
    hbm = pl.BlockSpec(memory_space=pl.ANY)
    dma = pltpu.SemaphoreType.DMA
    half = rows // 2
    chips = peers // 2
    all_rows = peers * slots
    all_new, picks, scaled, hidden_t, activation_t = pl.pallas_call(
        functools.partial(chain_kernel, sizes),
        out_shape=(
            jax.ShapeDtypeStruct((sections, TILE_ROWS, width), jnp.bfloat16),
            jax.ShapeDtypeStruct((micro * tokens, sections * TILE_ROWS), jnp.float32),
            jax.ShapeDtypeStruct((all_rows, features), jnp.bfloat16),
            jax.ShapeDtypeStruct((hid, all_rows), jnp.bfloat16),
            jax.ShapeDtypeStruct((hid, all_rows), jnp.bfloat16),
        ),
        in_specs=[hbm] * 7,
        out_specs=(vmem,) * 5,
        scratch_shapes=[
            pltpu.SMEM(route_tokens.shape, jnp.int32),
            pltpu.SMEM(gate.shape, jnp.float32),
            pltpu.SMEM(route_count.shape, jnp.int32),
            pltpu.VMEM(out_grad.shape, jnp.bfloat16),
            pltpu.VMEM(saved_u.shape, jnp.bfloat16),
            pltpu.VMEM((hid, features), jnp.bfloat16),
            pltpu.VMEM((hid, features), jnp.bfloat16),
            pltpu.VMEM((rows, width), jnp.bfloat16),
            pltpu.VMEM((rows, width), jnp.bfloat16),
            pltpu.VMEM((half, width), jnp.bfloat16),
            pltpu.VMEM((half, width), jnp.bfloat16),
            pltpu.VMEM((half, width), jnp.bfloat16),
            pltpu.VMEM((sections, TILE_ROWS, width), jnp.bfloat16),
            pltpu.VMEM((sections, 8, 128), jnp.int32),
            pltpu.VMEM((TILE_ROWS, width), jnp.float32),
            pltpu.VMEM((rows, hid), jnp.float32),
            dma((7,)),
            dma((CHUNKS, chips)),
            dma((CHUNKS, chips)),
            dma((CHUNKS,)),
            dma((CHUNKS,)),
            dma((CHUNKS,)),
            dma((CHUNKS,)),
            dma((CHUNKS, chips)),
            dma((CHUNKS, chips)),
            dma((sections,)),
            dma((sections,)),
            dma((CHUNKS, sections)),
            dma((CHUNKS, sections)),
        ],
        compiler_params=pltpu.CompilerParams(
            collective_id=0, has_side_effects=True, vmem_limit_bytes=48 * 1024 * 1024),
    )(route_tokens, gate, route_count, out_grad, saved_u, w_up_t, w_down)

    per_piece = CHUNKS
    block = width // per_piece
    return pl.pallas_call(
        functools.partial(gradient_kernel, (sections, slots, per_piece)),
        grid=(fold * per_piece,),
        out_shape=(
            jax.ShapeDtypeStruct((1, micro, tokens, features), jnp.bfloat16),
            jax.ShapeDtypeStruct((1, hid, features), jnp.bfloat16),
            jax.ShapeDtypeStruct((1, hid, features), jnp.bfloat16),
        ),
        in_specs=[
            pl.BlockSpec((hid, all_rows), lambda i: (0, 0)),
            pl.BlockSpec((hid, all_rows), lambda i: (0, 0)),
            pl.BlockSpec((all_rows, block), lambda i: (0, i)),
            pl.BlockSpec((1, micro, peers * cap, block), lambda i: (0, 0, 0, i)),
            pl.BlockSpec((micro, tokens, block), lambda i: (0, 0, i)),
            pl.BlockSpec((sections, TILE_ROWS, block), lambda i: (0, 0, i % per_piece)),
            pl.BlockSpec((micro * tokens, sections * TILE_ROWS), lambda i: (0, 0)),
        ],
        out_specs=(
            pl.BlockSpec((1, micro, tokens, block), lambda i: (0, 0, 0, i)),
            pl.BlockSpec((1, hid, block), lambda i: (0, 0, i)),
            pl.BlockSpec((1, hid, block), lambda i: (0, 0, i)),
        ),
        compiler_params=pltpu.CompilerParams(vmem_limit_bytes=32 * 1024 * 1024),
    )(hidden_t, activation_t, scaled, x_rows, out_grad, all_new, picks)


def solution(mesh):
    return jax.shard_map(
        functools.partial(per_device, mesh.shape["section"], mesh.shape["dp"]),
        mesh=mesh,
        in_specs=(
            P(None, "dp", None),
            P("section", None, None, None),
            P("section", None, None, "dp"),
            P("section", "dp", None),
            P("section", "dp", None),
            P("section", None, "dp"),
            P("section", None, "dp"),
            P("section", None, "dp"),
        ),
        out_specs=(
            P("section", None, "dp", None),
            P("section", "dp", None),
            P("section", "dp", None),
        ),
        check_vma=False,
    )
```

time: 91.2 us -> 90.8 us (level)
    pallas_call x1, Pallas kernels: 11.8 us -> 10.2 us  [per_device(): pl.pallas_call(functools.partial(gradient_kernel, (sections, slots, per_p...]
    pallas_call x1, Pallas kernels: 74.2 us -> 75.3 us  [per_device(): pl.pallas_call(functools.partial(chain_kernel, sizes), out_shape=(jax.Sha...]
where the time goes in v3:
time: 90.8 us; the launch traced here: 90.5 us
  Pallas kernels  85.6 us (94%)
  local copies, waits for them, and re-layouts  4.31 us (5%)
    pallas_call x1, Pallas kernels, per_device(): pl.pallas_call(functools.partial(chain_kernel, sizes), out_shape=(jax.Sha...  75.3 us
    pallas_call x1, Pallas kernels, per_device(): pl.pallas_call(functools.partial(gradient_kernel, (sections, slots, per_p...  10.2 us
    unnamed x11, local copies, waits for them, and re-layouts  4.31 us

profile of v3, /device:TPU:0, one launch (start us, length us, event | category | flops | bytes accessed | tf_op | source)
XLA Modules:
  0.0 90.5 jit_solution(3586638908644682692)
XLA Ops:
  0.6 0.7 copy.11.count_hbm
  1.4 0.0 copy-start
  1.4 1.4 %copy-done = bf16[2,64,6144]{2,1,0:T(8,128)(2,1)S(1)} copy-done((bf16[2,64,6144]{2,1,0:T(8,128)(2,1)S(1)}, bf16[2,64,6144]{2,1,0:T(8,128)(2,1)}, u32[]{:S(2)}) %copy-start) | copy-done | bytes 1572888
  2.8 0.0 copy-start.2
  2.8 0.8 copy-done.2
  3.6 0.0 copy-start.3
  3.6 0.7 copy-done.3
  4.3 0.0 copy-start.4
  4.3 0.7 copy-done.4
  4.9 0.0 copy-start.1
  4.9 75.3 %shard_map.103 = (bf16[4,16,1536]{2,1,0:T(8,128)(2,1)S(1)}, f32[128,64]{1,0:T(8,128)S(1)}, bf16[32,6144]{1,0:T(8,128)(2,1)S(1)}, bf16[672,32]{1,0:T(8,128)(2,1)S(1)}, bf16[672,32]{1,0:T(8,128)(2,1)S(1)}) custom-call(s32[1,2,2]{2,1,0:T(2,128)S(1)} %copy-done.3, f32[1,2,2]{2,1,0:T(2,128)S(1)} %copy-done.4, s32[1,2,1]{2,1,0:T(2,128)S(1)} %copy.11.count_hbm, ...), custom_call_target="tpu_custom_call" | custom-call | tf_op jit(solution)/shard_map/pallas_call | solution.py:397
  80.3 0.0 copy-done.1
  80.3 10.2 %shard_map.104 = (bf16[1,2,64,6144]{3,2,1,0:T(8,128)(2,1)}, bf16[1,672,6144]{2,1,0:T(8,128)(2,1)}, bf16[1,672,6144]{2,1,0:T(8,128)(2,1)}) custom-call(bf16[672,32]{1,0:T(8,128)(2,1)S(1)} %get-tuple-element.8.hidden_t_ref, bf16[672,32]{1,0:T(8,128)(2,1)S(1)} %get-tuple-element.9.activation_t_ref, bf16[32,6144]{1,0:T(8,128)(2,1)S(1)} %get-tuple-element.10.scaled_ref, ...), custom_call_target="tpu_custom_call" | custom-call | tf_op jit(solution)/shard_map/pallas_call | solution.py:445
Async XLA Ops:
  1.4 1.4 %copy-start = (bf16[2,64,6144]{2,1,0:T(8,128)(2,1)S(1)}, bf16[2,64,6144]{2,1,0:T(8,128)(2,1)}, u32[]{:S(2)}) copy-start(bf16[2,64,6144]{2,1,0:T(8,128)(2,1)} %grad_ref.1) | copy-start | bytes 4718596
  2.8 0.8 copy-start.2
  3.6 0.7 copy-start.3
  4.3 0.7 copy-start.4
  4.9 75.4 %copy-start.1 = (bf16[1,2,16,6144]{3,2,1,0:T(8,128)(2,1)S(1)}, bf16[1,2,16,6144]{3,2,1,0:T(8,128)(2,1)}, u32[]{:S(2)}) copy-start(bf16[1,2,16,6144]{3,2,1,0:T(8,128)(2,1)} %x_ref.1) | copy-start | bytes 1179652

commit v4 on v3

--- a/solution.py
+++ b/solution.py
@@ -9,7 +9,7 @@
 
 MESH = pl.DeviceIdType.MESH
 TILE_ROWS = 16
-CHUNKS = 3
+CHUNKS = 2
 
 
 def row_of_slot(index, peers, cap, micro):
@@ -437,10 +437,10 @@
             dma((CHUNKS, sections)),
         ],
         compiler_params=pltpu.CompilerParams(
-            collective_id=0, has_side_effects=True, vmem_limit_bytes=48 * 1024 * 1024),
+            collective_id=0, has_side_effects=True, vmem_limit_bytes=60 * 1024 * 1024),
     )(route_tokens, gate, route_count, out_grad, saved_u, w_up_t, w_down)
 
-    per_piece = CHUNKS
+    per_piece = 3
     block = width // per_piece
     return pl.pallas_call(
         functools.partial(gradient_kernel, (sections, slots, per_piece)),

time: 90.8 us -> 97.1 us (1.069)
  Pallas kernels: 85.6 us -> 90.3 us
  local copies, waits for them, and re-layouts: 4.31 us -> 5.89 us
    pallas_call x1, Pallas kernels: 75.3 us -> 80.1 us  [per_device(): pl.pallas_call(functools.partial(chain_kernel, sizes), out_shape=(jax.Sha...]
    unnamed x11 -> x15, local copies, waits for them, and re-layouts: 4.31 us -> 5.89 us
where the time goes in v4:
time: 97.1 us; the launch traced here: 96.9 us
  Pallas kernels  90.3 us (93%)
  local copies, waits for them, and re-layouts  5.89 us (6%)
    pallas_call x1, Pallas kernels, per_device(): pl.pallas_call(functools.partial(chain_kernel, sizes), out_shape=(jax.Sha...  80.1 us
    pallas_call x1, Pallas kernels, per_device(): pl.pallas_call(functools.partial(gradient_kernel, (sections, slots, per_p...  10.2 us
    unnamed x15, local copies, waits for them, and re-layouts  5.89 us

profile of v4, /device:TPU:0, one launch (start us, length us, event | category | flops | bytes accessed | tf_op | source)
XLA Modules:
  0.0 96.9 jit_solution(13147748529125588824)
XLA Ops:
  0.6 1.3 %copy.11.count_hbm = s32[1,2,1]{2,1,0:T(2,128)} copy(s32[1,2,1]{1,2,0:T(1,128)} %param.15) | data formatting | bytes 16 | tf_op args[7]
  1.9 0.0 copy-start
  1.9 0.0 copy-start.1
  1.9 80.1 %shard_map.103 = (bf16[4,16,1536]{2,1,0:T(8,128)(2,1)}, f32[128,64]{1,0:T(8,128)}, bf16[32,6144]{1,0:T(8,128)(2,1)}, bf16[672,32]{1,0:T(8,128)(2,1)}, bf16[672,32]{1,0:T(8,128)(2,1)}) custom-call(s32[1,2,2]{2,1,0:T(2,128)} %token_hbm.1, f32[1,2,2]{2,1,0:T(2,128)} %gate_hbm.1, s32[1,2,1]{2,1,0:T(2,128)} %copy.11.count_hbm, bf16[2,64,6144]{2,1,0:T(8,128)(2,1)} %grad_ref.1, ...), custom_call_target="tpu_custom_call" | custom-call | tf_op jit(solution)/shard_map/pallas_call | solution.py:397
  82.0 0.0 copy-done
  82.1 0.0 copy-done.1
  82.1 0.0 copy-start.2
  82.1 1.0 %copy-done.2 = bf16[32,6144]{1,0:T(8,128)(2,1)S(1)} copy-done((bf16[32,6144]{1,0:T(8,128)(2,1)S(1)}, bf16[32,6144]{1,0:T(8,128)(2,1)}, u32[]{:S(2)}) %copy-start.2) | copy-done | bytes 393240
  83.1 0.0 copy-start.3
  83.1 0.9 copy-done.3
  84.0 0.0 copy-start.4
  84.0 0.9 copy-done.4
  84.9 0.0 copy-start.5
  84.9 0.9 copy-done.5
  85.8 0.0 copy-start.6
  85.8 0.8 copy-done.6
  86.7 10.2 %shard_map.104 = (bf16[1,2,64,6144]{3,2,1,0:T(8,128)(2,1)}, bf16[1,672,6144]{2,1,0:T(8,128)(2,1)}, bf16[1,672,6144]{2,1,0:T(8,128)(2,1)}) custom-call(bf16[672,32]{1,0:T(8,128)(2,1)S(1)} %copy-done.4, bf16[672,32]{1,0:T(8,128)(2,1)S(1)} %copy-done.5, bf16[32,6144]{1,0:T(8,128)(2,1)S(1)} %copy-done.2, bf16[1,2,16,6144]{3,2,1,0:T(8,128)(2,1)S(1)} %copy-done.1, ...), custom_call_target="tpu_custom_call" | custom-call | tf_op jit(solution)/shard_map/pallas_call | solution.py:445
Async XLA Ops:
  1.9 80.1 %copy-start = (bf16[2,64,6144]{2,1,0:T(8,128)(2,1)S(1)}, bf16[2,64,6144]{2,1,0:T(8,128)(2,1)}, u32[]{:S(2)}) copy-start(bf16[2,64,6144]{2,1,0:T(8,128)(2,1)} %grad_ref.1) | copy-start | bytes 4718596
  1.9 80.1 %copy-start.1 = (bf16[1,2,16,6144]{3,2,1,0:T(8,128)(2,1)S(1)}, bf16[1,2,16,6144]{3,2,1,0:T(8,128)(2,1)}, u32[]{:S(2)}) copy-start(bf16[1,2,16,6144]{3,2,1,0:T(8,128)(2,1)} %x_ref.1) | copy-start | bytes 1179652
  82.1 1.0 %copy-start.2 = (bf16[32,6144]{1,0:T(8,128)(2,1)S(1)}, bf16[32,6144]{1,0:T(8,128)(2,1)}, u32[]{:S(2)}) copy-start(bf16[32,6144]{1,0:T(8,128)(2,1)} %get-tuple-element.10.scaled_ref) | copy-start | bytes 1179652
  83.1 0.9 copy-start.3
  84.0 0.9 copy-start.4
  84.9 0.9 copy-start.5
  85.8 0.8 copy-start.6

commit v5 on v4

--- a/solution.py
+++ b/solution.py
@@ -9,7 +9,7 @@
 
 MESH = pl.DeviceIdType.MESH
 TILE_ROWS = 16
-CHUNKS = 2
+CHUNKS = 6
 
 
 def row_of_slot(index, peers, cap, micro):
@@ -79,7 +79,7 @@
     for m in range(micro):
         for c in range(cap):
             flat.append(token_ref[0, m, c] + m * tokens)
-            weight.append(jnp.where(c < count_ref[0, m, 0], gate_ref[0, m, c], jnp.float32(0.0)))
+            weight.append(jnp.where(c < count_ref[0, 0, m], gate_ref[0, m, c], jnp.float32(0.0)))
     sent = []
     for k in range(slots):
         mine = flat[k]
@@ -205,8 +205,16 @@
             picks_ref[:, layer * TILE_ROWS:(layer + 1) * TILE_ROWS] = same
             found = jnp.maximum(found, jnp.max(same, axis=1, keepdims=True))
 
+    def find_slope():
+        source = row_of_slot(lax.broadcasted_iota(jnp.int32, (rows, slots * peers), 0), peers, cap, micro)
+        order = jnp.where(source == lax.broadcasted_iota(jnp.int32, (rows, slots * peers), 1), 1.0, 0.0)
+        pre = jnp.dot(order.astype(jnp.bfloat16), saved_ref[0].reshape(slots * peers, hid), preferred_element_type=jnp.float32)
+        sigmoid = jax.nn.sigmoid(pre)
+        slope_buf[...] = sigmoid * (1.0 + pre * (1.0 - sigmoid))
+
     @pl.when(has_above)
     def _():
+        find_slope()
         id_copy(above, above).wait_recv()
         prepare()
 
@@ -227,11 +235,9 @@
 
         lax.fori_loop(1, chips, send, 0)
 
-    source = row_of_slot(lax.broadcasted_iota(jnp.int32, (rows, slots * peers), 0), peers, cap, micro)
-    order = jnp.where(source == lax.broadcasted_iota(jnp.int32, (rows, slots * peers), 1), 1.0, 0.0)
-    pre = jnp.dot(order.astype(jnp.bfloat16), saved_ref[0].reshape(slots * peers, hid), preferred_element_type=jnp.float32)
-    sigmoid = jax.nn.sigmoid(pre)
-    slope_buf[...] = sigmoid * (1.0 + pre * (1.0 - sigmoid))
+    @pl.when(jnp.logical_not(has_above))
+    def _():
+        find_slope()
 
     down_copy.wait()
     up_copy.start()
@@ -294,19 +300,24 @@
             send_sums(chunk - 1)
     send_sums(CHUNKS - 1)
 
-    source = row_of_slot(lax.broadcasted_iota(jnp.int32, (slots * peers, rows), 1), peers, cap, micro)
-    order = jnp.where(source == lax.broadcasted_iota(jnp.int32, (slots * peers, rows), 0), 1.0, 0.0)
-    piece_lane = lax.broadcasted_iota(jnp.int32, (slots * peers, rows), 1) % TILE_ROWS // slots
-    for piece in range(fold):
-        mine = jnp.where(piece_lane == piece, order, 0.0).astype(jnp.bfloat16)
-        if piece == 0:
-            hidden_t_ref[...] = jnp.dot(mine, hidden, preferred_element_type=jnp.float32).T.astype(jnp.bfloat16)
-        scaled_ref[:, piece * width:(piece + 1) * width] = jnp.dot(
-            mine, gbuf[...], preferred_element_type=jnp.float32).astype(jnp.bfloat16)
-    for layer in range(sections):
-        @pl.when(layer > section)
-        def _():
-            all_new_ref[layer] = new_buf[layer]
+    def keep_rows():
+        source = row_of_slot(lax.broadcasted_iota(jnp.int32, (slots * peers, rows), 1), peers, cap, micro)
+        order = jnp.where(source == lax.broadcasted_iota(jnp.int32, (slots * peers, rows), 0), 1.0, 0.0)
+        piece_lane = lax.broadcasted_iota(jnp.int32, (slots * peers, rows), 1) % TILE_ROWS // slots
+        for piece in range(fold):
+            mine = jnp.where(piece_lane == piece, order, 0.0).astype(jnp.bfloat16)
+            if piece == 0:
+                hidden_t_ref[...] = jnp.dot(mine, hidden, preferred_element_type=jnp.float32).T.astype(jnp.bfloat16)
+            scaled_ref[:, piece * width:(piece + 1) * width] = jnp.dot(
+                mine, gbuf[...], preferred_element_type=jnp.float32).astype(jnp.bfloat16)
+        for layer in range(sections):
+            @pl.when(layer > section)
+            def _():
+                all_new_ref[layer] = new_buf[layer]
+
+    @pl.when(section == 0)
+    def _():
+        keep_rows()
 
     alike = jnp.where(id_col[:, :1] == id_row[:1, :], 1.0, 0.0).astype(jnp.bfloat16)
     for chunk in range(CHUNKS):
@@ -330,6 +341,11 @@
             for chunk in range(CHUNKS):
                 new_copy(chunk, section, target).start()
     all_new_ref[section] = new_buf[section]
+
+    @pl.when(section > 0)
+    def _():
+        keep_rows()
+
 
     @pl.when(jnp.logical_not(has_above))
     def _():
@@ -408,7 +424,7 @@
         scratch_shapes=[
             pltpu.SMEM(route_tokens.shape, jnp.int32),
             pltpu.SMEM(gate.shape, jnp.float32),
-            pltpu.SMEM(route_count.shape, jnp.int32),
+            pltpu.SMEM((1, 1, micro), jnp.int32),
             pltpu.VMEM(out_grad.shape, jnp.bfloat16),
             pltpu.VMEM(saved_u.shape, jnp.bfloat16),
             pltpu.VMEM((hid, features), jnp.bfloat16),
@@ -438,9 +454,9 @@
         ],
         compiler_params=pltpu.CompilerParams(
             collective_id=0, has_side_effects=True, vmem_limit_bytes=60 * 1024 * 1024),
-    )(route_tokens, gate, route_count, out_grad, saved_u, w_up_t, w_down)
-
-    per_piece = 3
+    )(route_tokens, gate, route_count.transpose(0, 2, 1), out_grad, saved_u, w_up_t, w_down)
+
+    per_piece = 2
     block = width // per_piece
     return pl.pallas_call(
         functools.partial(gradient_kernel, (sections, slots, per_piece)),
@@ -464,7 +480,7 @@
             pl.BlockSpec((1, hid, block), lambda i: (0, 0, i)),
             pl.BlockSpec((1, hid, block), lambda i: (0, 0, i)),
         ),
-        compiler_params=pltpu.CompilerParams(vmem_limit_bytes=32 * 1024 * 1024),
+        compiler_params=pltpu.CompilerParams(vmem_limit_bytes=60 * 1024 * 1024),
     )(hidden_t, activation_t, scaled, x_rows, out_grad, all_new, picks)
 
 

time: 97.1 us -> 90.3 us (0.930)
  local copies, waits for them, and re-layouts: 5.89 us -> 0 us
  Pallas kernels: 90.3 us -> 89.3 us
    unnamed x15 -> x0, local copies, waits for them, and re-layouts: 5.89 us -> none
    pallas_call x1, Pallas kernels: 80.1 us -> 78.1 us  [per_device(): pl.pallas_call(functools.partial(chain_kernel, sizes), out_shape=(jax.Sha...]
    pallas_call x1, Pallas kernels: 10.2 us -> 11.3 us  [per_device(): pl.pallas_call(functools.partial(gradient_kernel, (sections, slots, per_p...]
where the time goes in v5:
time: 90.3 us; the launch traced here: 90 us
  Pallas kernels  89.3 us (99%)
    pallas_call x1, Pallas kernels, per_device(): pl.pallas_call(functools.partial(chain_kernel, sizes), out_shape=(jax.Sha...  78.1 us
    pallas_call x1, Pallas kernels, per_device(): pl.pallas_call(functools.partial(gradient_kernel, (sections, slots, per_p...  11.3 us

profile of v5, /device:TPU:0, one launch (start us, length us, event | category | flops | bytes accessed | tf_op | source)
XLA Modules:
  0.0 90.0 jit_solution(10844443679876475939)
XLA Ops:
  0.6 78.1 %shard_map.103 = (bf16[4,16,1536]{2,1,0:T(8,128)(2,1)}, f32[128,64]{1,0:T(8,128)}, bf16[32,6144]{1,0:T(8,128)(2,1)}, bf16[672,32]{1,0:T(8,128)(2,1)}, bf16[672,32]{1,0:T(8,128)(2,1)}) custom-call(s32[1,2,2]{2,1,0:T(2,128)} %token_hbm.1, f32[1,2,2]{2,1,0:T(2,128)} %gate_hbm.1, s32[1,1,2]{2,1,0:T(1,128)} %bitcast.1, bf16[2,64,6144]{2,1,0:T(8,128)(2,1)} %grad_ref.1, ...), custom_call_target="tpu_custom_call" | custom-call | tf_op jit(solution)/shard_map/pallas_call | solution.py:413
  78.7 11.3 %shard_map.104 = (bf16[1,2,64,6144]{3,2,1,0:T(8,128)(2,1)}, bf16[1,672,6144]{2,1,0:T(8,128)(2,1)}, bf16[1,672,6144]{2,1,0:T(8,128)(2,1)}) custom-call(bf16[672,32]{1,0:T(8,128)(2,1)} %get-tuple-element.8.hidden_t_ref, bf16[672,32]{1,0:T(8,128)(2,1)} %get-tuple-element.9.activation_t_ref, bf16[32,6144]{1,0:T(8,128)(2,1)} %get-tuple-element.10.scaled_ref, ...), custom_call_target="tpu_custom_call" | custom-call | tf_op jit(solution)/shard_map/pallas_call | solution.py:461

commit v6 on v5

--- a/solution.py
+++ b/solution.py
@@ -9,7 +9,7 @@
 
 MESH = pl.DeviceIdType.MESH
 TILE_ROWS = 16
-CHUNKS = 6
+CHUNKS = 3
 
 
 def row_of_slot(index, peers, cap, micro):
@@ -456,7 +456,7 @@
             collective_id=0, has_side_effects=True, vmem_limit_bytes=60 * 1024 * 1024),
     )(route_tokens, gate, route_count.transpose(0, 2, 1), out_grad, saved_u, w_up_t, w_down)
 
-    per_piece = 2
+    per_piece = 3
     block = width // per_piece
     return pl.pallas_call(
         functools.partial(gradient_kernel, (sections, slots, per_piece)),

time: 90.3 us -> 89.1 us (0.987)
  Pallas kernels: 89.3 us -> 88.1 us
    pallas_call x1, Pallas kernels: 78.1 us -> 75.1 us  [per_device(): pl.pallas_call(functools.partial(chain_kernel, sizes), out_shape=(jax.Sha...]
    pallas_call x1, Pallas kernels: 11.3 us -> 13 us  [per_device(): pl.pallas_call(functools.partial(gradient_kernel, (sections, slots, per_p...]
where the time goes in v6:
time: 89.1 us; the launch traced here: 88.7 us
  Pallas kernels  88.1 us (99%)
    pallas_call x1, Pallas kernels, per_device(): pl.pallas_call(functools.partial(chain_kernel, sizes), out_shape=(jax.Sha...  75.1 us
    pallas_call x1, Pallas kernels, per_device(): pl.pallas_call(functools.partial(gradient_kernel, (sections, slots, per_p...  13 us

profile of v6, /device:TPU:0, one launch (start us, length us, event | category | flops | bytes accessed | tf_op | source)
XLA Modules:
  0.0 88.7 jit_solution(13233435011684710840)
XLA Ops:
  0.6 75.1 %shard_map.103 = (bf16[4,16,1536]{2,1,0:T(8,128)(2,1)}, f32[128,64]{1,0:T(8,128)}, bf16[32,6144]{1,0:T(8,128)(2,1)}, bf16[672,32]{1,0:T(8,128)(2,1)}, bf16[672,32]{1,0:T(8,128)(2,1)}) custom-call(s32[1,2,2]{2,1,0:T(2,128)} %token_hbm.1, f32[1,2,2]{2,1,0:T(2,128)} %gate_hbm.1, s32[1,1,2]{2,1,0:T(1,128)} %bitcast.1, bf16[2,64,6144]{2,1,0:T(8,128)(2,1)} %grad_ref.1, ...), custom_call_target="tpu_custom_call" | custom-call | tf_op jit(solution)/shard_map/pallas_call | solution.py:413
  75.7 13.0 %shard_map.104 = (bf16[1,2,64,6144]{3,2,1,0:T(8,128)(2,1)}, bf16[1,672,6144]{2,1,0:T(8,128)(2,1)}, bf16[1,672,6144]{2,1,0:T(8,128)(2,1)}) custom-call(bf16[672,32]{1,0:T(8,128)(2,1)} %get-tuple-element.8.hidden_t_ref, bf16[672,32]{1,0:T(8,128)(2,1)} %get-tuple-element.9.activation_t_ref, bf16[32,6144]{1,0:T(8,128)(2,1)} %get-tuple-element.10.scaled_ref, ...), custom_call_target="tpu_custom_call" | custom-call | tf_op jit(solution)/shard_map/pallas_call | solution.py:461
